TPU v7x, 256 devices: a whole 4x4x8 slice. The times are simulated.
256 devices in a mesh: seq: 64 (over z, x, core), ch: 4 (over y).
Axes of the slice: x: 4, y: 4, z: 8, core: 2. Of those that a mesh axis runs over, the one named last changes fastest.
Arguments:
- layer_input: bfloat16 [16384, 4096], P('seq', 'ch'), may hold values from -6 to 6
- query_gate: bfloat16 [16384, 512], P('seq', 'ch'), may hold values from -6 to 6
- key_gate: bfloat16 [16384, 512], P('seq', 'ch'), may hold values from -6 to 6
- value_field: bfloat16 [16384, 512], P('seq', 'ch'), may hold values from -6 to 6
- out_grad: bfloat16 [16384, 512], P('seq', 'ch'), may hold values from -0.125 to 0.125
- filter_taps: float32 [16384, 512], P('seq', 'ch'), may hold values from -0.046875 to 0.046875
Outputs:
- grad_in_proj: float32 [1536, 4096], P('seq', 'ch')
- grad_filter: float32 [16384, 512], P('seq', 'ch')
All inputs are finite; a program needn't handle non-finite values.
Results may differ from a plain program's by a relative error of at most 0.0029.
Values may be sent and summed in bfloat16 or wider, within the bound.
No kernel may reach another device: no remote copies, remote signals or barrier semaphores. Data moves between devices by JAX's collectives and lax.ppermute only.
A program may use at most 128 MiB of HBM per device.

v0:
```python
import math

import jax
import jax.numpy as jnp
from jax import lax
from jax.sharding import PartitionSpec as P

highest = lax.Precision.HIGHEST


def dft_tables(rows_full, columns):
    total = rows_full * columns
    half_rows = rows_full // 2
    freq_rows = jnp.arange(rows_full, dtype=jnp.int32)
    time_rows = jnp.arange(half_rows, dtype=jnp.int32)
    time_cols = jnp.arange(columns, dtype=jnp.int32)
    first_angle = (
        2.0
        * math.pi
        / rows_full
        * (freq_rows[:, None] * time_rows[None, :] % rows_full).astype(jnp.float32)
    )
    twist_angle = (
        2.0
        * math.pi
        / total
        * (freq_rows[:, None] * time_cols[None, :] % total).astype(jnp.float32)
    )
    second_angle = (
        2.0
        * math.pi
        / columns
        * (time_cols[:, None] * time_cols[None, :] % columns).astype(jnp.float32)
    )
    return (
        jnp.cos(first_angle),
        -jnp.sin(first_angle),
        jnp.cos(twist_angle),
        -jnp.sin(twist_angle),
        jnp.cos(second_angle),
        -jnp.sin(second_angle),
    )


def right_product(source, matrix):
    return jnp.einsum("ckm,mj->ckj", source, matrix, precision=highest)


def left_product(matrix, source):
    return jnp.einsum("kh,chm->ckm", matrix, source, precision=highest)


def left_adjoint(matrix, source):
    return jnp.einsum("kh,ckm->chm", matrix, source, precision=highest)


def second_section(first_real, first_imag, tables):
    twist_real, twist_imag, outer_real, outer_imag = (tables[2], tables[3], tables[4], tables[5])
    mixed_real = first_real * twist_real - first_imag * twist_imag
    mixed_imag = first_real * twist_imag + first_imag * twist_real
    spec_real = right_product(mixed_real, outer_real) - right_product(mixed_imag, outer_imag)
    spec_imag = right_product(mixed_real, outer_imag) + right_product(mixed_imag, outer_real)
    return (spec_real, spec_imag)


def forward_real(signal, tables):
    return second_section(left_product(tables[0], signal), left_product(tables[1], signal), tables)


def inverse_mix(spec_real, spec_imag, tables):
    back_real = right_product(spec_real, tables[4]) + right_product(spec_imag, tables[5])
    back_imag = right_product(spec_imag, tables[4]) - right_product(spec_real, tables[5])
    turned_real = back_real * tables[2] + back_imag * tables[3]
    turned_imag = back_imag * tables[2] - back_real * tables[3]
    return (turned_real, turned_imag)


def inverse_real(spec_real, spec_imag, tables, inverse_scale):
    turned_real, turned_imag = inverse_mix(spec_real, spec_imag, tables)
    return (
        left_adjoint(tables[0], turned_real) + left_adjoint(tables[1], turned_imag)
    ) * inverse_scale


def per_channel(fields):
    gated_field, upstream, taps = fields
    item_count = gated_field.shape[1]
    length = gated_field.shape[2]
    columns = math.gcd(length, 256)
    rows_full = 2 * length // columns
    grid_shape = (item_count, rows_full // 2, columns)
    tables = dft_tables(rows_full, columns)
    inverse_scale = 1.0 / (rows_full * columns)
    gated_grid = gated_field.reshape(grid_shape)
    upstream_grid = upstream.reshape(grid_shape)
    taps_real, taps_imag = forward_real(taps.reshape(grid_shape), tables)
    value_real, value_imag = forward_real(gated_grid, tables)
    grad_real, grad_imag = forward_real(upstream_grid, tables)
    conv_real = taps_real * value_real - taps_imag * value_imag
    conv_imag = taps_real * value_imag + taps_imag * value_real
    back_real = taps_real * grad_real + taps_imag * grad_imag
    back_imag = taps_real * grad_imag - taps_imag * grad_real
    lag_real = value_real * grad_real + value_imag * grad_imag
    lag_imag = value_real * grad_imag - value_imag * grad_real
    conv_out = inverse_real(conv_real, conv_imag, tables, inverse_scale)
    gated_grad = inverse_real(back_real, back_imag, tables, inverse_scale)
    lag_grad = inverse_real(lag_real, lag_imag, tables, inverse_scale)
    flat_shape = (1, item_count, length)
    return (
        lax.all_to_all(
            conv_out.reshape(flat_shape), "seq", split_axis=2, concat_axis=0, tiled=True
        ),
        lax.all_to_all(
            gated_grad.reshape(flat_shape), "seq", split_axis=2, concat_axis=0, tiled=True
        ),
        lax.all_to_all(
            lag_grad.reshape(flat_shape), "seq", split_axis=2, concat_axis=0, tiled=True
        ),
    )


def on_device(layer_input, query_gate, key_gate, value_field, out_grad, filter_taps):
    shards = lax.axis_size("seq")
    tok_rows, local_ch = query_gate.shape
    per_group = local_ch // shards
    key_wide = key_gate.astype(jnp.float32)
    value_wide = value_field.astype(jnp.float32)
    grad_wide = out_grad.astype(jnp.float32)
    gated_field = key_wide * value_wide
    upstream = grad_wide * query_gate.astype(jnp.float32)

    def to_groups(source):
        return source.T.reshape(shards, per_group, tok_rows)

    def to_rows(source):
        return source.reshape(local_ch, tok_rows).T

    conv_back, gated_back, lag_back = per_channel(
        (
            lax.all_to_all(to_groups(gated_field), "seq", split_axis=0, concat_axis=2, tiled=True),
            lax.all_to_all(to_groups(upstream), "seq", split_axis=0, concat_axis=2, tiled=True),
            lax.all_to_all(to_groups(filter_taps), "seq", split_axis=0, concat_axis=2, tiled=True),
        )
    )
    conv_out = to_rows(conv_back)
    gated_grad = to_rows(gated_back)
    grad_filter = to_rows(lag_back)
    grad_query = (grad_wide * conv_out).astype(jnp.bfloat16)
    grad_key = (gated_grad * value_wide).astype(jnp.bfloat16)
    grad_value = (gated_grad * key_wide).astype(jnp.bfloat16)
    full_query, full_key, full_value = (
        lax.all_gather(grad_query, "ch", axis=1, tiled=True),
        lax.all_gather(grad_key, "ch", axis=1, tiled=True),
        lax.all_gather(grad_value, "ch", axis=1, tiled=True),
    )
    stacked = jnp.concatenate([full_query, full_key, full_value], axis=1)
    grad_in_proj = lax.psum_scatter(
        lax.dot_general(
            stacked, layer_input, (((0,), (0,)), ((), ())), preferred_element_type=jnp.float32
        ),
        "seq",
        scatter_dimension=0,
        tiled=True,
    )
    return (grad_in_proj, grad_filter)


def solution(mesh):
    return jax.shard_map(
        on_device,
        mesh=mesh,
        in_specs=(
            P("seq", "ch"),
            P("seq", "ch"),
            P("seq", "ch"),
            P("seq", "ch"),
            P("seq", "ch"),
            P("seq", "ch"),
        ),
        out_specs=(P("seq", "ch"), P("seq", "ch")),
        check_vma=False,
    )
```

profile of v0, /device:TPU:8, one launch (start us, length us, event | category | flops | bytes accessed | tf_op | source)
XLA Modules:
  0.0 524.1 jit_solution(18128237155837381320)
XLA Ops:
  7.2 1.0 copy.76
  8.2 0.9 copy.96
  9.2 0.7 reshape.89
  9.9 11.9 %all-to-all-start.3 = ((f32[64,2,256]{2,1,0:T(2,128)}), f32[64,2,256]{2,1,0:T(2,128)S(1)}, u32[]{:S(2)}, u32[]{:S(2)}) async-start(f32[64,2,256]{2,1,0:T(2,128)} %reshape.89), calls=%async_computation.3 | async-start | bytes 262144 | tf_op jit(solution)/shard_map/all_to_all | solution.py:141
  21.8 0.9 copy.79
  22.8 0.9 copy.80
  24.4 1.0 copy.77
  25.5 0.7 reshape.83
  26.9 6.0 %all-to-all-done.3 = f32[64,2,256]{2,1,0:T(2,128)S(1)} async-done(((f32[64,2,256]{2,1,0:T(2,128)}), f32[64,2,256]{2,1,0:T(2,128)S(1)}, u32[]{:S(2)}, u32[]{:S(2)}) %all-to-all-start.3) | async-done | bytes 131104 | tf_op jit(solution)/shard_map/all_to_all | solution.py:141
  32.9 4.6 all-to-all-start.1
  38.8 1.5 fusion.19
  40.3 1.5 fusion.41
  41.8 6.9 %all-to-all-done.1 = f32[64,2,256]{2,1,0:T(2,128)S(1)} async-done(((f32[64,2,256]{2,1,0:T(2,128)}), f32[64,2,256]{2,1,0:T(2,128)S(1)}, u32[]{:S(2)}, u32[]{:S(2)}) %all-to-all-start.1) | async-done | bytes 131104 | tf_op jit(solution)/shard_map/all_to_all | solution.py:140
  48.7 5.1 all-to-all-start
  55.0 1.5 fusion.24
  56.5 2.2 fusion.49
  58.7 5.7 %all-to-all-done = f32[64,2,256]{2,1,0:T(2,128)S(1)} async-done(((f32[64,2,256]{2,1,0:T(2,128)}), f32[64,2,256]{2,1,0:T(2,128)S(1)}, u32[]{:S(2)}, u32[]{:S(2)}) %all-to-all-start) | async-done | bytes 131104 | tf_op jit(solution)/shard_map/all_to_all | solution.py:142
  65.6 1.4 fusion.26
  67.0 1.4 fusion.51
  68.3 1.5 convolution_add_fusion.2
  69.8 1.5 convolution_subtract_fusion.2
  71.3 2.6 convolution_subtract_fusion.4
  74.0 1.4 convolution_add_fusion.5
  75.3 1.4 convolution_subtract_fusion.5
  76.7 1.6 multiply_add_fusion
  78.3 1.5 fusion.36
  79.9 1.5 fusion.38
  81.4 1.6 convolution_subtract_fusion.1
  83.0 1.6 convolution_add_fusion.1
  84.5 1.7 fusion.43
  86.3 1.5 fusion.45
  87.8 1.6 convolution_subtract_fusion.3
  89.3 1.6 convolution_add_fusion.3
  92.0 4.6 copy.145
  97.2 74.4 %reduce.2 = f32[16384,2]{1,0:T(8,128)} reduce(f32[16384,1,2]{2,1,0:T(1,128)} %bitcast.175, f32[]{:T(128)} %broadcast.211), dimensions={1}, to_apply=%bitcast.156.reduce_sub_computation | reduce | bytes 262148
  171.7 8.6 %reshape.102 = f32[64,1,512]{2,1,0:T(1,128)} reshape(f32[16384,2]{1,0:T(8,128)} %reduce.2) | data formatting | bytes 262144
  180.3 4.6 all-to-all-start.2
  186.0 4.6 copy.146
  190.6 74.4 %reduce = f32[16384,2]{1,0:T(8,128)} reduce(f32[16384,1,2]{2,1,0:T(1,128)} %bitcast.176, f32[]{:T(128)} %broadcast.211), dimensions={1}, to_apply=%bitcast.154.reduce_sub_computation | reduce | bytes 262148
  265.1 8.2 %reshape.100 = f32[64,1,512]{2,1,0:T(1,128)} reshape(f32[16384,2]{1,0:T(8,128)} %reduce) | data formatting | bytes 262144
  273.3 10.3 %all-to-all-start.4 = ((f32[64,1,512]{2,1,0:T(1,128)}), f32[64,1,512]{2,1,0:T(1,128)S(1)}, u32[]{:S(2)}, u32[]{:S(2)}) async-start(f32[64,1,512]{2,1,0:T(1,128)} %reshape.100), calls=%async_computation.4 | async-start | bytes 262144 | tf_op jit(solution)/shard_map/all_to_all | solution.py:113
  283.6 0.9 reduce.3
  284.6 15.1 %reshape.103 = f32[16384,1,2]{2,1,0:T(1,128)} reshape(f32[64,512]{1,0:T(8,128)S(1)} %reduce.3) | data formatting | bytes 262144
  299.7 5.4 %copy.95 = f32[1,2,64,256]{3,1,2,0:T(2,128)S(1)} copy(f32[1,2,64,256]{1,3,2,0:T(8,128)} %bitcast.178) | data formatting | bytes 262144 | tf_op jit(solution)/shard_map/all_to_all | solution.py:110
  305.1 12.6 %all_gather.9 = bf16[256,512]{0,1:T(8,128)(2,1)S(1)} all-gather(bf16[256,128]{0,1:T(8,128)(2,1)S(1)} %fusion.79), channel_id=1, replica_groups=mesh['seq'=64,'ch'=4] {'ch'}, dimensions={1}, use_global_device_ids=true | all-gather | bytes 327680 | tf_op jit(solution)/shard_map/all_gather | solution.py:152
  317.7 0.9 reduce.1
  318.7 14.9 %reshape.101 = f32[16384,1,2]{2,1,0:T(1,128)} reshape(f32[64,512]{1,0:T(8,128)S(1)} %reduce.1) | data formatting | bytes 262144
  333.6 5.4 %copy.109 = f32[1,2,64,256]{3,1,2,0:T(2,128)S(1)} copy(f32[1,2,64,256]{1,3,2,0:T(8,128)} %bitcast.179) | data formatting | bytes 262144 | tf_op jit(solution)/shard_map/all_to_all | solution.py:113
  339.1 12.3 %all_gather.10 = bf16[256,512]{0,1:T(8,128)(2,1)S(1)} all-gather(bf16[256,128]{0,1:T(8,128)(2,1)S(1)} %get-tuple-element.16), channel_id=1, replica_groups=mesh['seq'=64,'ch'=4] {'ch'}, dimensions={1}, use_global_device_ids=true | all-gather | bytes 327680 | tf_op jit(solution)/shard_map/all_gather | solution.py:153
  351.3 12.5 %all_gather.11 = bf16[256,512]{0,1:T(8,128)(2,1)S(1)} all-gather(bf16[256,128]{0,1:T(8,128)(2,1)S(1)} %get-tuple-element.17), channel_id=1, replica_groups=mesh['seq'=64,'ch'=4] {'ch'}, dimensions={1}, use_global_device_ids=true | all-gather | bytes 327680 | tf_op jit(solution)/shard_map/all_gather | solution.py:154
  363.8 3.6 fusion.6
  367.4 1.5 fusion.34
  369.0 1.5 fusion.32
  370.5 1.6 convolution_add_fusion
  372.1 1.6 convolution_subtract_fusion
  374.8 4.9 copy.147
  379.7 74.5 %reduce.4 = f32[16384,2]{1,0:T(8,128)} reduce(f32[16384,1,2]{2,1,0:T(1,128)} %bitcast.177, f32[]{:T(128)} %broadcast.211), dimensions={1}, to_apply=%bitcast.158.reduce_sub_computation | reduce | bytes 262148
  454.2 7.6 %reshape.104 = f32[64,1,512]{2,1,0:T(1,128)S(1)} reshape(f32[16384,2]{1,0:T(8,128)} %reduce.4) | data formatting | bytes 262144
  461.8 21.2 %all_to_all.90 = f32[64,1,512]{2,1,0:T(1,128)S(1)} all-to-all(f32[64,1,512]{2,1,0:T(1,128)S(1)} %reshape.104), channel_id=1, replica_groups=mesh['seq'=64,'ch'=4] {'seq'}, dimensions={0} | all-to-all | bytes 262144 | tf_op jit(solution)/shard_map/all_to_all | solution.py:116
  483.0 0.9 reduce.5
  484.0 14.9 %reshape.105 = f32[16384,1,2]{2,1,0:T(1,128)} reshape(f32[64,512]{1,0:T(8,128)S(1)} %reduce.5) | data formatting | bytes 262144
  498.9 5.4 %copy.117 = f32[1,2,64,256]{3,1,2,0:T(2,128)S(1)} copy(f32[1,2,64,256]{1,3,2,0:T(8,128)} %bitcast.180) | data formatting | bytes 262144 | tf_op jit(solution)/shard_map/all_to_all | solution.py:116
  504.4 0.8 copy.118
  505.1 11.9 %reduce-scatter.4.cloned.1.call-done = f32[24,1024]{1,0:T(8,128)} async-done(((f32[1536,1024]{1,0:T(8,128)}), f32[24,1024]{1,0:T(8,128)}) %reduce-scatter.4.cloned.1.call-update) | async-done | bytes 98320
  (30 shorter events, 9.4 us)
Async XLA Ops:
  7.2 356.6 %copy-start = (bf16[256,1024]{1,0:T(8,128)(2,1)S(1)}, bf16[256,1024]{1,0:T(8,128)(2,1)}, u32[]{:S(2)}) copy-start(bf16[256,1024]{1,0:T(8,128)(2,1)} %param.6) | copy-start | bytes 1572868
  9.9 23.0 %all-to-all-start.3 = ((f32[64,2,256]{2,1,0:T(2,128)}), f32[64,2,256]{2,1,0:T(2,128)S(1)}, u32[]{:S(2)}, u32[]{:S(2)}) async-start(f32[64,2,256]{2,1,0:T(2,128)} %reshape.89), calls=%async_computation.3 | async-start | bytes 262144 | tf_op jit(solution)/shard_map/all_to_all | solution.py:141
  32.9 15.8 %all-to-all-start.1 = ((f32[64,2,256]{2,1,0:T(2,128)}), f32[64,2,256]{2,1,0:T(2,128)S(1)}, u32[]{:S(2)}, u32[]{:S(2)}) async-start(f32[64,2,256]{2,1,0:T(2,128)} %reshape.85), calls=%async_computation.1 | async-start | bytes 262144 | tf_op jit(solution)/shard_map/all_to_all | solution.py:140
  48.7 15.8 %all-to-all-start = ((f32[64,2,256]{2,1,0:T(2,128)}), f32[64,2,256]{2,1,0:T(2,128)S(1)}, u32[]{:S(2)}, u32[]{:S(2)}) async-start(f32[64,2,256]{2,1,0:T(2,128)} %reshape.83), calls=%async_computation | async-start | bytes 262144 | tf_op jit(solution)/shard_map/all_to_all | solution.py:142
  180.3 93.0 %all-to-all-start.2 = ((f32[64,1,512]{2,1,0:T(1,128)}), f32[64,1,512]{2,1,0:T(1,128)S(1)}, u32[]{:S(2)}, u32[]{:S(2)}) async-start(f32[64,1,512]{2,1,0:T(1,128)} %reshape.102), calls=%async_computation.2 | async-start | bytes 262144 | tf_op jit(solution)/shard_map/all_to_all | solution.py:110
  273.3 44.4 %all-to-all-start.4 = ((f32[64,1,512]{2,1,0:T(1,128)}), f32[64,1,512]{2,1,0:T(1,128)S(1)}, u32[]{:S(2)}, u32[]{:S(2)}) async-start(f32[64,1,512]{2,1,0:T(1,128)} %reshape.100), calls=%async_computation.4 | async-start | bytes 262144 | tf_op jit(solution)/shard_map/all_to_all | solution.py:113
  283.6 233.4 %reduce-scatter.4.cloned.1.call-start = ((), (), s32[]{:S(2)}) async-start(), calls=%async_computation.7 | async-start | bytes 6389760
Sparse Core Ops, SparseCore 0:
  367.6 149.4 reduce-scatter.3
where the time goes:
time: 531 us; the launch traced here: 524 us
  other arithmetic  227 us (43%)
  local copies, waits for them, and re-layouts  108 us (20%)
  blocking collectives  58.5 us (11%)
  matrix products  48.7 us (9%)
  starting transfers between devices  36.6 us (7%)
  waiting for transfers between devices  30.5 us (6%)
  between operations  14.7 us (3%)
    unnamed x3, other arithmetic  223 us
    unnamed x14, local copies, waits for them, and re-layouts  74.5 us
    dot_general x24, matrix products, right_product(): return jnp.einsum('ckm,mj->ckj', source, matrix, precision=highest)  38.1 us
    all_to_all x1, blocking collectives, per_channel(): lax.all_to_all(lag_grad.reshape(flat_shape), 'seq', split_axis=2, concat_...  21.2 us
    all_gather x1, blocking collectives, on_device(): lax.all_gather(grad_query, 'ch', axis=1, tiled=True)  12.6 us
    all_gather x1, blocking collectives, on_device(): lax.all_gather(grad_value, 'ch', axis=1, tiled=True)  12.5 us
    all_gather x1, blocking collectives, on_device(): lax.all_gather(grad_key, 'ch', axis=1, tiled=True)  12.3 us
    all_to_all x1, starting transfers between devices, on_device(): lax.all_to_all(to_groups(upstream), 'seq', split_axis=0, concat_axis=2, t...  11.9 us
  transfers between devices with their start and end apart: 6, of which 4 were waited for; matrix products, arithmetic and copies ran while one was open for 46% of the time, Pallas kernels for 0%

commit v1 on v0

v1 whole, which is shorter than its diff:
```python
import jax
import jax.numpy as jnp
import numpy as np
from jax import lax
from jax.experimental import pallas as pl
from jax.experimental.pallas import tpu as pltpu
from jax.sharding import Mesh
from jax.sharding import PartitionSpec as P

NZ, NX, NCORE, NP, NY = 8, 4, 2, 8, 4
BLOCKS, BLOCK_LEN, SHARD_CH = 64, 256, 128
BINS, TRANSFORM = 64, 32768
bf16, f32 = jnp.bfloat16, jnp.float32


def split_np(table):
    high = table.astype(np.float32).astype(jnp.bfloat16)
    low = (table - high.astype(np.float64)).astype(jnp.bfloat16)
    return high, low


def pack_order():
    order = np.zeros((8 * BLOCKS, 4 * SHARD_CH), np.float32)
    for z in range(NZ):
        for p in range(NP):
            for s in range(2):
                for j in range(2):
                    for half in range(2):
                        row = (8 * z + p) * 8 + 4 * s + 2 * j + half
                        order[row, (2 * s + half) * SHARD_CH + 64 * j + 8 * p + z] = 1.0
    return order.astype(jnp.bfloat16)


def tables():
    bins = np.arange(BINS, dtype=np.float64) + 0.5
    held = np.array([8 * z + p for p in range(NP) for z in range(NZ)], np.float64)
    lag = np.arange(BLOCK_LEN, dtype=np.float64)
    first = 2.0 * np.pi / 128.0 * bins[:, None] * held[None, :]
    twist = 2.0 * np.pi / TRANSFORM * bins[:, None] * lag[None, :]
    second = 2.0 * np.pi / BLOCK_LEN * ((lag[:, None] * lag[None, :]) % BLOCK_LEN)
    ahead_high, ahead_low = split_np(np.concatenate([np.cos(first), -np.sin(first)], axis=0))
    ahead = np.concatenate([ahead_high, ahead_high, ahead_low], axis=1)
    back = np.concatenate([np.cos(first).T, -np.sin(first).T], axis=1) * (2.0 / TRANSFORM)
    back_high, back_low = split_np(back)
    back = np.concatenate([back_high, back_high, back_low], axis=1)
    cosine, sine = np.cos(second), np.sin(second)
    outer_high, outer_low = split_np(np.block([[cosine, -sine], [sine, cosine]]))
    turn = np.stack([np.cos(twist), -np.sin(twist)]).astype(np.float32)
    return ahead, back, turn, outer_high, outer_low


def split(value):
    high = value.astype(bf16)
    low = (value - high.astype(f32)).astype(bf16)
    return high, low


def product(left, right, dims):
    return lax.dot_general(left, right, (dims, ((), ())), preferred_element_type=f32)


def pack_kernel(key_ref, value_ref, grad_ref, query_ref, taps_ref, order_ref, out_ref):
    taps_high, taps_low = split(taps_ref[...])
    order = order_ref[...]

    def tile(first, second):
        wide = jnp.concatenate(
            [first[:128], first[128:], second[:128], second[128:]], axis=1
        )
        return product(order, wide, ((1,), (1,))).reshape(BLOCKS, 8, 128)

    out_ref[...] = jnp.concatenate(
        [
            tile(key_ref[...], value_ref[...]),
            tile(grad_ref[...], query_ref[...]),
            tile(taps_high, taps_low),
        ],
        axis=1,
    ).astype(bf16)


def conv_kernel(
    got_ref, ahead_ref, back_ref, turn_ref, high_ref, low_ref, out_ref, lag_ref, rows_ref, lag_rows_ref
):
    rows_ref[...] = got_ref[...].astype(f32).reshape(BLOCKS * 24, 128)

    def field(number):
        parts = []
        for p in range(NP):
            parts.append(
                jnp.concatenate(
                    [rows_ref[pl.ds(p * 24 + number * 4 + r, 8, stride=192), :] for r in range(4)],
                    axis=1,
                )
            )
        return jnp.concatenate(parts, axis=0)

    key, value, grad, query = field(0), field(1), field(2), field(3)
    taps = field(4) + field(5)
    signals = jnp.concatenate([taps, key * value, grad * query], axis=1)
    sig_high, sig_low = split(signals)
    mixed = product(
        ahead_ref[...], jnp.concatenate([sig_high, sig_low, sig_high], axis=0), ((1,), (0,))
    )
    turn_real, turn_imag = turn_ref[0], turn_ref[1]
    turned = []
    for block in range(6):
        real = mixed[:BINS, 256 * block : 256 * (block + 1)]
        imag = mixed[BINS:, 256 * block : 256 * (block + 1)]
        turned.append(
            jnp.concatenate(
                [real * turn_real - imag * turn_imag, real * turn_imag + imag * turn_real], axis=1
            )
        )
    outer_high, outer_low = high_ref[...], low_ref[...]

    def outer(source, dims):
        high, low = split(source)
        return (
            product(high, outer_high, dims)
            + product(low, outer_high, dims)
            + product(high, outer_low, dims)
        )

    spec = outer(jnp.concatenate(turned, axis=0), ((1,), (0,)))
    tr, ti = spec[:128, :256], spec[:128, 256:]
    vr, vi = spec[128:256, :256], spec[128:256, 256:]
    ur, ui = spec[256:, :256], spec[256:, 256:]
    mixes = jnp.concatenate(
        [
            jnp.concatenate([tr * vr - ti * vi, tr * vi + ti * vr], axis=1),
            jnp.concatenate([tr * ur + ti * ui, tr * ui - ti * ur], axis=1),
            jnp.concatenate([vr * ur + vi * ui, vr * ui - vi * ur], axis=1),
        ],
        axis=0,
    )
    home = outer(mixes, ((1,), (1,)))
    reals, imags = [], []
    for block in range(6):
        real = home[BINS * block : BINS * (block + 1), :256]
        imag = home[BINS * block : BINS * (block + 1), 256:]
        reals.append(real * turn_real + imag * turn_imag)
        imags.append(imag * turn_real - real * turn_imag)
    untwisted = jnp.concatenate(
        [jnp.concatenate(reals, axis=1), jnp.concatenate(imags, axis=1)], axis=0
    )
    home_high, home_low = split(untwisted)
    result = product(
        back_ref[...], jnp.concatenate([home_high, home_low, home_high], axis=0), ((1,), (0,))
    )
    conv_out, gated_grad, lag_grad = result[:, :512], result[:, 512:1024], result[:, 1024:]
    stacked = (grad * conv_out, gated_grad * value, gated_grad * key)
    for p in range(NP):
        block = jnp.concatenate(
            [
                field_rows[8 * p : 8 * p + 8, 128 * lane : 128 * lane + 128]
                for field_rows in stacked
                for lane in range(4)
            ],
            axis=0,
        ).astype(bf16)
        for y in range(NY):
            out_ref[p * NY + y] = block
    lag_high = lag_grad.astype(bf16).astype(f32)
    lag_low = lag_grad - lag_high
    for level, part in ((0, lag_high), (1, lag_low)):
        for p in range(NP):
            for r in range(4):
                lag_rows_ref[pl.ds(p * 8 + 4 * level + r, 8, stride=64), :] = part[
                    8 * p : 8 * p + 8, 128 * r : 128 * r + 128
                ]
    lag_ref[...] = lag_rows_ref[...].reshape(BLOCKS, 8, 128)


def share_kernel(got_ref, input_ref, lag_ref, out_ref, rows_ref, held_ref, sums_ref, done):
    copy = pltpu.make_async_copy(input_ref, held_ref, done)
    copy.start()
    rows_ref[...] = got_ref[...].astype(f32).reshape(32 * 96, 128)
    left = []
    for z in range(NZ):
        tiles = []
        for kind in range(3):
            for y in range(NY):
                for j in range(2):
                    lane = kind * 4 + j * 2
                    tiles.append(
                        jnp.concatenate(
                            [
                                rows_ref[pl.ds(y * 96 + (lane + half) * 8 + z, 8, stride=384), :]
                                for half in range(2)
                            ],
                            axis=1,
                        )
                    )
        left.append(jnp.concatenate(tiles, axis=0).astype(bf16))
    left = jnp.concatenate(left, axis=1)
    copy.wait()
    total = product(left, held_ref[...], ((1,), (0,)))
    for lane in range(8):
        sums_ref[pl.ds(lane, 192, stride=8), :] = total[:, 128 * lane : 128 * lane + 128]
    out_ref[...] = jnp.concatenate(
        [sums_ref[...].reshape(BLOCKS, 24, 128), lag_ref[...]], axis=1
    ).astype(bf16)


def finish_kernel(got_ref, proj_ref, filter_ref, sums_ref, rows_ref):
    wide = got_ref[...].astype(f32)
    sums_ref[...] = (
        wide.reshape(NZ, NP, 32, 128)[:, :, :24, :].sum(axis=1).reshape(NZ * 24, 128)
    )
    for e in range(3):
        for lane in range(8):
            proj_ref[8 * e : 8 * e + 8, 128 * lane : 128 * lane + 128] = sums_ref[
                pl.ds(8 * e + lane, 8, stride=24), :
            ]
    rows_ref[...] = wide.reshape(BLOCKS * 32, 128)
    for half in range(2):
        tiles = []
        for j in range(2):
            for p in range(NP):
                start = p * 32 + 24 + 2 * j + half
                tiles.append(
                    rows_ref[pl.ds(start, 8, stride=256), :]
                    + rows_ref[pl.ds(start + 4, 8, stride=256), :]
                )
        filter_ref[128 * half : 128 * half + 128, :] = jnp.concatenate(tiles, axis=0).T


VMEM = pltpu.VMEM


def call(kernel, name, args, outs, scratch, spaces=None):
    spaces = spaces or [pltpu.VMEM] * len(args)
    return pl.pallas_call(
        kernel,
        out_shape=outs,
        in_specs=[pl.BlockSpec(memory_space=space) for space in spaces],
        out_specs=jax.tree.map(lambda _: pl.BlockSpec(memory_space=pltpu.VMEM), outs),
        scratch_shapes=scratch,
        compiler_params=pltpu.CompilerParams(vmem_limit_bytes=48 * 2**20),
        name=name,
    )(*args)


def on_device(layer_input, query_gate, key_gate, value_field, out_grad, filter_taps):
    held_input = lax.all_gather(layer_input, "z", axis=0, tiled=True)
    ahead, back, turn, outer_high, outer_low = (jnp.asarray(t) for t in tables())
    packed = call(
        pack_kernel,
        "pack",
        (key_gate, value_field, out_grad, query_gate, filter_taps, jnp.asarray(pack_order())),
        jax.ShapeDtypeStruct((BLOCKS, 24, 128), bf16),
        [],
    )
    fields = lax.all_to_all(packed, ("z", "x", "core"), split_axis=0, concat_axis=0, tiled=True)
    grads, lags = call(
        conv_kernel,
        "conv",
        (fields, ahead, back, turn, outer_high, outer_low),
        (
            jax.ShapeDtypeStruct((NP * NY, 96, 128), bf16),
            jax.ShapeDtypeStruct((BLOCKS, 8, 128), f32),
        ),
        [VMEM((BLOCKS * 24, 128), f32), VMEM((BLOCKS * 8, 128), f32)],
    )
    stacked = lax.all_to_all(grads, ("x", "core", "y"), split_axis=0, concat_axis=0, tiled=True)
    shares = call(
        share_kernel,
        "share",
        (stacked, held_input, lags),
        jax.ShapeDtypeStruct((BLOCKS, 32, 128), bf16),
        [
            VMEM((32 * 96, 128), f32),
            VMEM((2048, 1024), bf16),
            VMEM((1536, 128), f32),
            pltpu.SemaphoreType.DMA,
        ],
        [pltpu.VMEM, pl.ANY, pltpu.VMEM],
    )
    parts = lax.all_to_all(shares, ("z", "x", "core"), split_axis=0, concat_axis=0, tiled=True)
    return call(
        finish_kernel,
        "finish",
        (parts,),
        (
            jax.ShapeDtypeStruct((24, 1024), f32),
            jax.ShapeDtypeStruct((BLOCK_LEN, SHARD_CH), f32),
        ),
        [VMEM((NZ * 24, 128), f32), VMEM((BLOCKS * 32, 128), f32)],
    )


def solution(mesh):
    fine = Mesh(mesh.devices.reshape(NZ, NX, NCORE, NY), ("z", "x", "core", "y"))
    spec = P(("z", "x", "core"), "y")
    return jax.shard_map(
        on_device,
        mesh=fine,
        in_specs=(spec,) * 6,
        out_specs=(spec, spec),
        check_vma=False,
    )
```

time: 531 us -> 115 us (0.22)
  the two profiles are of different devices: /device:TPU:8 before, /device:TPU:1 now
where the time goes in v1:
time: 115 us
  blocking collectives  78.4 us (68%)
  between operations  14.1 us (12%)
  local copies, waits for them, and re-layouts  12.1 us (11%)
  Pallas kernels  6.32 us (5%)
  waiting for transfers between devices  3.65 us (3%)
    all_to_all x1, blocking collectives, on_device(): lax.all_to_all(packed, ('z', 'x', 'core'), split_axis=0, concat_axis=0, t...  32 us
    all_to_all x1, blocking collectives, on_device(): lax.all_to_all(shares, ('z', 'x', 'core'), split_axis=0, concat_axis=0, t...  25.5 us
    all_to_all x1, blocking collectives, on_device(): lax.all_to_all(grads, ('x', 'core', 'y'), split_axis=0, concat_axis=0, ti...  20.9 us
    unnamed x24, local copies, waits for them, and re-layouts  12.1 us
    pallas_call x4, Pallas kernels, call(): pl.pallas_call(kernel, out_shape=outs, in_specs=[pl.BlockSpec(memory_spac...  6.32 us
    all_gather x1, waiting for transfers between devices, on_device(): held_input = lax.all_gather(layer_input, 'z', axis=0, tiled=True)  2.97 us
  transfers between devices with their start and end apart: 1, of which 1 were waited for; matrix products, arithmetic and copies ran while one was open for 0% of the time, Pallas kernels for 3%

profile of v1, /device:TPU:1, one launch (start us, length us, event | category | flops | bytes accessed | tf_op | source)
XLA Modules:
  0.0 114.6 jit_solution(11157791844793960202)
XLA Ops:
  7.2 0.0 all-gather.2.cloned.1.call-start
  7.2 0.7 all-gather.2.cloned.1.call-update
  7.9 0.0 copy-start.3
  7.9 1.0 copy-done.3
  8.9 0.0 copy-start.4
  8.9 0.9 copy-done.4
  9.8 0.0 copy-start.6
  9.9 0.8 copy-done.6
  10.7 0.0 copy-start.7
  10.7 0.8 copy-done.7
  11.5 0.0 copy-start.8
  11.5 0.8 copy-done.8
  12.4 0.0 copy-start.9
  12.4 0.8 copy-done.9
  13.2 0.6 pack.1
  13.8 32.0 %all_to_all.15.got_ref = bf16[64,24,128]{2,1,0:T(8,128)(2,1)S(1)} all-to-all(bf16[64,24,128]{2,1,0:T(8,128)(2,1)S(1)} %pack.1), channel_id=1, replica_groups=mesh['z'=8,'x'=4,'core'=2,'y'=4] {'z','x','core'}, dimensions={0} | all-to-all | bytes 786432 | tf_op jit(solution)/shard_map/all_to_all | solution.py:255
  45.8 0.0 copy-start.1
  45.8 1.1 copy-done.1
  46.9 0.0 copy-start.2
  46.9 1.0 copy-done.2
  47.9 0.0 copy-start.5
  47.9 0.9 copy-done.5
  48.8 0.0 copy-start.10
  48.8 0.8 copy-done.10
  49.7 0.0 copy-start.11
  49.7 0.8 copy-done.11
  50.5 2.6 %conv.1 = (bf16[32,96,128]{2,1,0:T(8,128)(2,1)S(1)}, f32[64,8,128]{2,1,0:T(8,128)S(1)}) custom-call(bf16[64,24,128]{2,1,0:T(8,128)(2,1)S(1)} %all_to_all.15.got_ref, bf16[128,192]{1,0:T(8,128)(2,1)S(1)} %copy-done.10, bf16[64,384]{1,0:T(8,128)(2,1)S(1)} %copy-done.11, f32[2,64,256]{2,1,0:T(8,128)S(1)} %copy-done.5, bf16[512,512]{1,0:T(8,128)(2,1)S(1)} %copy-done.1, ...), custom_call_target="tpu_custom_call" | custom-call | tf_op jit(solution)/shard_map/conv/pallas_call | solution.py:234
  53.0 20.9 %all_to_all.16.got_ref = bf16[32,96,128]{2,1,0:T(8,128)(2,1)S(1)} all-to-all(bf16[32,96,128]{2,1,0:T(8,128)(2,1)S(1)} %get-tuple-element.4), channel_id=1, replica_groups=mesh['z'=8,'x'=4,'core'=2,'y'=4] {'x','core','y'}, dimensions={0} | all-to-all | bytes 1572864 | tf_op jit(solution)/shard_map/all_to_all | solution.py:266
  73.9 3.0 %all-gather.2.cloned.1.call-done.input_ref = bf16[2048,1024]{1,0:T(8,128)(2,1)} async-done(((bf16[256,1024]{1,0:T(8,128)(2,1)}), bf16[2048,1024]{1,0:T(8,128)(2,1)}) %all-gather.2.cloned.1.call-update) | async-done | bytes 4194320 | tf_op jit(solution)/shard_map/all_gather | solution.py:246
  76.9 0.0 copy-start
  76.9 2.2 %copy-done = bf16[2048,1024]{1,0:T(8,128)(2,1)S(1)} copy-done((bf16[2048,1024]{1,0:T(8,128)(2,1)S(1)}, bf16[2048,1024]{1,0:T(8,128)(2,1)}, u32[]{:S(2)}) %copy-start) | copy-done | bytes 4194328
  79.1 2.3 %share.1 = bf16[64,32,128]{2,1,0:T(8,128)(2,1)S(1)} custom-call(bf16[32,96,128]{2,1,0:T(8,128)(2,1)S(1)} %all_to_all.16.got_ref, bf16[2048,1024]{1,0:T(8,128)(2,1)S(1)} %copy-done, f32[64,8,128]{2,1,0:T(8,128)S(1)} %get-tuple-element.5.lag_ref), custom_call_target="tpu_custom_call" | custom-call | tf_op jit(solution)/shard_map/share/pallas_call | solution.py:234
  81.3 25.5 %all_to_all.17.got_ref = bf16[64,32,128]{2,1,0:T(8,128)(2,1)S(1)} all-to-all(bf16[64,32,128]{2,1,0:T(8,128)(2,1)S(1)} %share.1), channel_id=1, replica_groups=mesh['z'=8,'x'=4,'core'=2,'y'=4] {'z','x','core'}, dimensions={0} | all-to-all | bytes 1048576 | tf_op jit(solution)/shard_map/all_to_all | solution.py:280
  106.8 0.9 finish.1
Async XLA Ops:
  7.2 69.7 %all-gather.2.cloned.1.call-start = ((), (), s32[]{:S(2)}) async-start(), calls=%async_computation.3 | async-start | bytes 4718592 | tf_op jit(solution)/shard_map/all_gather | solution.py:246
  7.9 1.0 copy-start.3
  8.9 0.9 copy-start.4
  9.8 0.8 copy-start.6
  10.7 0.8 copy-start.7
  11.5 0.8 copy-start.8
  12.4 0.8 copy-start.9
  45.8 1.1 copy-start.1
  46.9 1.0 copy-start.2
  47.9 0.9 copy-start.5
  48.8 0.8 copy-start.10
  49.7 0.8 copy-start.11
  76.9 2.2 %copy-start = (bf16[2048,1024]{1,0:T(8,128)(2,1)S(1)}, bf16[2048,1024]{1,0:T(8,128)(2,1)}, u32[]{:S(2)}) copy-start(bf16[2048,1024]{1,0:T(8,128)(2,1)} %all-gather.2.cloned.1.call-done.input_ref) | copy-start | bytes 12582916
Sparse Core Ops, SparseCore 0:
  9.8 67.0 all-gather.1

commit v2 on v1

v2 whole, which is shorter than its diff:
```python
import jax
import jax.numpy as jnp
import numpy as np
from jax import lax
from jax.experimental import pallas as pl
from jax.experimental.pallas import tpu as pltpu
from jax.sharding import Mesh
from jax.sharding import PartitionSpec as P

NZ, NX, NCORE, NA, NY = 8, 4, 2, 8, 4
BLOCKS, BLOCK_LEN, SHARD_CH = 64, 256, 128
BINS, TRANSFORM = 64, 32768
bf16, f32 = jnp.bfloat16, jnp.float32


def split_np(table):
    high = table.astype(np.float32).astype(jnp.bfloat16)
    low = (table - high.astype(np.float64)).astype(jnp.bfloat16)
    return high, low


def pack_order():
    order = np.zeros((8 * BLOCKS, 4 * SHARD_CH), np.float32)
    for i in range(BLOCKS):
        for s in range(2):
            for j in range(2):
                for half in range(2):
                    row = i * 8 + 4 * s + 2 * j + half
                    order[row, (2 * s + half) * SHARD_CH + 64 * j + i] = 1.0
    return order.astype(jnp.bfloat16)


def tables():
    bins = np.arange(BINS, dtype=np.float64) + 0.5
    held = np.arange(BLOCKS, dtype=np.float64)
    lag = np.arange(BLOCK_LEN, dtype=np.float64)
    first = 2.0 * np.pi / 128.0 * bins[:, None] * held[None, :]
    twist = 2.0 * np.pi / TRANSFORM * bins[:, None] * lag[None, :]
    second = 2.0 * np.pi / BLOCK_LEN * ((lag[:, None] * lag[None, :]) % BLOCK_LEN)
    ahead_high, ahead_low = split_np(np.concatenate([np.cos(first), -np.sin(first)], axis=0))
    back = np.concatenate([np.cos(first).T, -np.sin(first).T], axis=1) * (2.0 / TRANSFORM)
    back_high, back_low = split_np(back)
    cosine, sine = np.cos(second), np.sin(second)
    outer = split_np(np.block([[cosine, -sine], [sine, cosine]]))
    turn = split_np(np.concatenate([np.cos(twist), -np.sin(twist)], axis=1))
    ahead = np.concatenate([ahead_high, ahead_high, ahead_low], axis=1)
    back = np.concatenate([back_high, back_high, back_low], axis=1)
    ahead = np.pad(ahead, ((0, 0), (0, 512 - ahead.shape[1])))
    back = np.pad(back, ((0, 0), (0, 512 - back.shape[1])))
    return np.concatenate([*outer, *turn, ahead, back], axis=0)


def split(value):
    high = value.astype(bf16)
    low = (value - high.astype(f32)).astype(bf16)
    return high, low


def product(left, right, dims):
    return lax.dot_general(left, right, (dims, ((), ())), preferred_element_type=f32)


def fetch(pairs, done):
    copies = [
        pltpu.make_async_copy(source, target, done.at[number])
        for number, (source, target) in enumerate(pairs)
    ]
    for copy in copies:
        copy.start()
    return copies


def pack_kernel(key_in, value_in, grad_in, query_in, taps_in, order_in, out_ref, *scratch):
    *held, done = scratch
    key_ref, value_ref, grad_ref, query_ref, taps_ref, order_ref = held
    sources = (key_in, value_in, grad_in, query_in, taps_in, order_in)
    for copy in fetch(zip(sources, held, strict=True), done):
        copy.wait()
    taps_high, taps_low = split(taps_ref[...])
    order = order_ref[...]

    def tile(first, second):
        wide = jnp.concatenate(
            [first[:128], first[128:], second[:128], second[128:]], axis=1
        )
        return product(order, wide, ((1,), (1,))).reshape(BLOCKS, 8, 128)

    out_ref[...] = jnp.concatenate(
        [
            tile(key_ref[...], value_ref[...]),
            tile(grad_ref[...], query_ref[...]),
            tile(taps_high, taps_low),
        ],
        axis=1,
    ).astype(bf16)


def conv_kernel(got_ref, table_ref, out_ref, lag_ref, rows_ref, lag_rows_ref):
    rows_ref[...] = got_ref[...].astype(f32).reshape(BLOCKS * 24, 128)

    def field(number):
        parts = []
        for z in range(NZ):
            parts.append(
                jnp.concatenate(
                    [rows_ref[pl.ds(z * 192 + number * 4 + r, 8, stride=24), :] for r in range(4)],
                    axis=1,
                )
            )
        return jnp.concatenate(parts, axis=0)

    key, value, grad, query = field(0), field(1), field(2), field(3)
    taps = field(4) + field(5)
    signals = jnp.concatenate([taps, key * value, grad * query], axis=1)
    sig_high, sig_low = split(signals)
    mixed = product(
        table_ref[1152:1280, :192], jnp.concatenate([sig_high, sig_low, sig_high], axis=0), ((1,), (0,))
    )
    turn = table_ref[1024:1088].astype(f32) + table_ref[1088:1152].astype(f32)
    turn_real, turn_imag = turn[:, :256], turn[:, 256:]
    turned = []
    for block in range(6):
        real = mixed[:BINS, 256 * block : 256 * (block + 1)]
        imag = mixed[BINS:, 256 * block : 256 * (block + 1)]
        turned.append(
            jnp.concatenate(
                [real * turn_real - imag * turn_imag, real * turn_imag + imag * turn_real], axis=1
            )
        )
    outer_high, outer_low = table_ref[:512], table_ref[512:1024]

    def outer(source, dims):
        high, low = split(source)
        return (
            product(high, outer_high, dims)
            + product(low, outer_high, dims)
            + product(high, outer_low, dims)
        )

    spec = outer(jnp.concatenate(turned, axis=0), ((1,), (0,)))
    tr, ti = spec[:128, :256], spec[:128, 256:]
    vr, vi = spec[128:256, :256], spec[128:256, 256:]
    ur, ui = spec[256:, :256], spec[256:, 256:]
    mixes = jnp.concatenate(
        [
            jnp.concatenate([tr * vr - ti * vi, tr * vi + ti * vr], axis=1),
            jnp.concatenate([tr * ur + ti * ui, tr * ui - ti * ur], axis=1),
            jnp.concatenate([vr * ur + vi * ui, vr * ui - vi * ur], axis=1),
        ],
        axis=0,
    )
    home = outer(mixes, ((1,), (1,)))
    reals, imags = [], []
    for block in range(6):
        real = home[BINS * block : BINS * (block + 1), :256]
        imag = home[BINS * block : BINS * (block + 1), 256:]
        reals.append(real * turn_real + imag * turn_imag)
        imags.append(imag * turn_real - real * turn_imag)
    untwisted = jnp.concatenate(
        [jnp.concatenate(reals, axis=1), jnp.concatenate(imags, axis=1)], axis=0
    )
    home_high, home_low = split(untwisted)
    result = product(
        table_ref[1280:1344, :384], jnp.concatenate([home_high, home_low, home_high], axis=0), ((1,), (0,))
    )
    conv_out, gated_grad, lag_grad = result[:, :512], result[:, 512:1024], result[:, 1024:]
    stacked = (grad * conv_out, gated_grad * value, gated_grad * key)
    for z in range(NZ):
        block = jnp.concatenate(
            [
                field_rows[8 * z : 8 * z + 8, 128 * lane : 128 * lane + 128]
                for field_rows in stacked
                for lane in range(4)
            ],
            axis=0,
        ).astype(bf16)
        for y in range(NY):
            out_ref[z * NY + y] = block
    lag_high = lag_grad.astype(bf16).astype(f32)
    lag_low = lag_grad - lag_high
    for level, part in ((0, lag_high), (1, lag_low)):
        for z in range(NZ):
            for r in range(4):
                lag_rows_ref[pl.ds(z * 64 + 4 * level + r, 8, stride=8), :] = part[
                    8 * z : 8 * z + 8, 128 * r : 128 * r + 128
                ]
    lag_ref[...] = lag_rows_ref[...].reshape(BLOCKS, 8, 128)


def share_kernel(got_ref, lag_ref, *rest):
    inputs, (out_ref, rows_ref, held_ref, sums_ref, done) = rest[:14], rest[14:]
    x, core = lax.axis_index("x"), lax.axis_index("core")
    across = lax.rem(x + 2, NX)
    beside = x + 1 - 2 * lax.rem(x, 2)
    half = BLOCK_LEN // 2
    pairs = []
    for swap, unit in ((0, core), (1, 1 - core)):
        for source, (place, offset, length) in zip(
            inputs[7 * swap : 7 * swap + 7],
            (
                (x, 0, BLOCK_LEN),
                (beside, half, half),
                (NX - 1 - x, 0, half),
                (beside, 0, half),
                (NX - 1 - x, half, half),
                (across, 0, half),
                (across, half, half),
            ),
            strict=True,
        ):
            start = pl.multiple_of((NCORE * place + unit) * BLOCK_LEN + offset, half)
            pairs.append((source, held_ref.at[pl.ds(start, length)]))
    copies = fetch(pairs, done)
    rows_ref[...] = got_ref[...].astype(f32).reshape(32 * 96, 128)
    left = []
    for a in range(NA):
        tiles = []
        for kind in range(3):
            for y in range(NY):
                for j in range(2):
                    lane = kind * 4 + j * 2
                    tiles.append(
                        jnp.concatenate(
                            [
                                rows_ref[pl.ds(y * 96 + (lane + half) * 8 + a, 8, stride=384), :]
                                for half in range(2)
                            ],
                            axis=1,
                        )
                    )
        left.append(jnp.concatenate(tiles, axis=0).astype(bf16))
    left = jnp.concatenate(left, axis=1)
    for copy in copies:
        copy.wait()
    total = product(left, held_ref[...], ((1,), (0,)))
    for lane in range(8):
        sums_ref[pl.ds(lane, 192, stride=8), :] = total[:, 128 * lane : 128 * lane + 128]
    out_ref[...] = jnp.concatenate(
        [sums_ref[...].reshape(BLOCKS, 24, 128), lag_ref[...]], axis=1
    ).astype(bf16)


def finish_kernel(got_ref, proj_ref, filter_ref, sums_ref, rows_ref):
    wide = got_ref[...].astype(f32)
    sums_ref[...] = (
        wide.reshape(NZ, NA, 32, 128)[:, :, :24, :].sum(axis=0).reshape(NA * 24, 128)
    )
    for e in range(3):
        for lane in range(8):
            proj_ref[8 * e : 8 * e + 8, 128 * lane : 128 * lane + 128] = sums_ref[
                pl.ds(8 * e + lane, 8, stride=24), :
            ]
    rows_ref[...] = wide.reshape(BLOCKS * 32, 128)
    for half in range(2):
        tiles = []
        for j in range(2):
            for z in range(NZ):
                start = z * 256 + 24 + 2 * j + half
                tiles.append(
                    rows_ref[pl.ds(start, 8, stride=32), :]
                    + rows_ref[pl.ds(start + 4, 8, stride=32), :]
                )
        filter_ref[128 * half : 128 * half + 128, :] = jnp.concatenate(tiles, axis=0).T


VMEM, HBM = pltpu.VMEM, pltpu.HBM


def call(kernel, name, args, spaces, outs, scratch, grant):
    return pl.pallas_call(
        kernel,
        out_shape=outs,
        in_specs=[pl.BlockSpec(memory_space=space) for space in spaces],
        out_specs=jax.tree.map(lambda _: pl.BlockSpec(memory_space=VMEM), outs),
        scratch_shapes=scratch,
        compiler_params=pltpu.CompilerParams(vmem_limit_bytes=grant * 2**20),
        name=name,
    )(*args)


def held_like(arrays):
    return [VMEM(array.shape, array.dtype) for array in arrays] + [
        pltpu.SemaphoreType.DMA((len(arrays),))
    ]


def on_device(layer_input, query_gate, key_gate, value_field, out_grad, filter_taps):
    pairs, rings = [(0, 1), (1, 0), (2, 3), (3, 2)], [(0, 3), (3, 0), (1, 2), (2, 1)]
    half = BLOCK_LEN // 2
    near_low = lax.ppermute(layer_input[half:], "x", pairs)
    far_high = lax.ppermute(layer_input[:half], "x", rings)
    sources = (key_gate, value_field, out_grad, query_gate, filter_taps, jnp.asarray(pack_order()))
    packed = call(
        pack_kernel,
        "pack",
        sources,
        [HBM] * 6,
        jax.ShapeDtypeStruct((BLOCKS, 24, 128), bf16),
        held_like(sources),
        60,
    )
    fields = lax.all_to_all(packed, ("z", "x", "core"), split_axis=0, concat_axis=0, tiled=True)
    grads, lags = call(
        conv_kernel,
        "conv",
        (fields, jnp.asarray(tables())),
        [VMEM] * 2,
        (
            jax.ShapeDtypeStruct((NZ * NY, 96, 128), bf16),
            jax.ShapeDtypeStruct((BLOCKS, 8, 128), f32),
        ),
        [VMEM((BLOCKS * 24, 128), f32), VMEM((BLOCKS * 8, 128), f32)],
        32,
    )
    grads, held, near_low, far_high = lax.optimization_barrier(
        (grads, layer_input, near_low, far_high)
    )
    near_high = lax.ppermute(held[:half], "x", pairs)
    far_low = lax.ppermute(held[half:], "x", rings)
    across_high = lax.ppermute(far_high, "x", pairs)
    across_low = lax.ppermute(near_low, "x", rings)
    own = (layer_input, near_low, far_high, near_high, far_low, across_high, across_low)
    other = [lax.ppermute(block, "core", [(0, 1), (1, 0)]) for block in own]
    stacked = lax.all_to_all(grads, ("z", "y"), split_axis=0, concat_axis=0, tiled=True)
    shares = call(
        share_kernel,
        "share",
        (stacked, lags, *own, *other),
        [VMEM, VMEM] + [pl.ANY] * 14,
        jax.ShapeDtypeStruct((BLOCKS, 32, 128), bf16),
        [
            VMEM((32 * 96, 128), f32),
            VMEM((2048, 1024), bf16),
            VMEM((1536, 128), f32),
            pltpu.SemaphoreType.DMA((14,)),
        ],
        52,
    )
    parts = lax.all_to_all(shares, ("z", "x", "core"), split_axis=0, concat_axis=0, tiled=True)
    return call(
        finish_kernel,
        "finish",
        (parts,),
        [VMEM],
        (
            jax.ShapeDtypeStruct((24, 1024), f32),
            jax.ShapeDtypeStruct((BLOCK_LEN, SHARD_CH), f32),
        ),
        [VMEM((NA * 24, 128), f32), VMEM((BLOCKS * 32, 128), f32)],
        32,
    )


def solution(mesh):
    fine = Mesh(mesh.devices.reshape(NZ, NX, NCORE, NY), ("z", "x", "core", "y"))
    spec = P(("z", "x", "core"), "y")
    return jax.shard_map(
        on_device,
        mesh=fine,
        in_specs=(spec,) * 6,
        out_specs=(spec, spec),
        check_vma=False,
    )
```

time: 115 us -> 93.6 us (0.81)
  blocking collectives: 78.4 us -> 25.4 us
  starting transfers between devices: 0.04 us -> 31.7 us
  waiting for transfers between devices: 3.65 us -> 22.3 us
  between operations: 14.1 us -> 0.77 us
  local copies, waits for them, and re-layouts: 12.1 us -> 1.51 us
  Pallas kernels: 6.32 us -> 11.5 us
    all_to_all x2 -> x0, blocking collectives: 52.9 us -> none  [the longest x1 32 us: on_device(): lax.all_to_all(packed, ('z', 'x', 'core'), split_axis=0, concat_axis=0, t...]
    all_to_all x0 -> x2, starting transfers between devices: none -> 19.5 us  [the longest x1 13 us: on_device(): lax.all_to_all(packed, ('z', 'x', 'core'), split_axis=0, concat_axis=0, t...]
    all_to_all x0 -> x2, waiting for transfers between devices: none -> 13.8 us  [the longest x1 11.7 us: on_device(): lax.all_to_all(packed, ('z', 'x', 'core'), split_axis=0, concat_axis=0, t...]
    ppermute x0 -> x13, starting transfers between devices: none -> 12.2 us  [the longest x7 5.99 us: on_device(): other = [lax.ppermute(block, 'core', [(0, 1), (1, 0)]) for block in own]]
    unnamed x24 -> x16, local copies, waits for them, and re-layouts: 12.1 us -> 0.74 us
    ppermute x0 -> x13, waiting for transfers between devices: none -> 8.55 us  [the longest x1 3.59 us: on_device(): across_low = lax.ppermute(near_low, 'x', rings)]
    pallas_call x4, Pallas kernels: 6.32 us -> 11.5 us  [call(): pl.pallas_call(kernel, out_shape=outs, in_specs=[pl.BlockSpec(memory_spac...]
    all_gather x1 -> x0, waiting for transfers between devices: 2.97 us -> none  [on_device(): held_input = lax.all_gather(layer_input, 'z', axis=0, tiled=True)]
  transfers between devices with their start and end apart: 1 -> 15, of which waited for: 1 -> 5; matrix products, arithmetic and copies ran while one was open for 0% -> 1% of each run, Pallas kernels for 3% -> 3%
where the time goes in v2:
time: 93.6 us; the launch traced here: 93.2 us
  starting transfers between devices  31.7 us (34%)
  blocking collectives  25.4 us (27%)
  waiting for transfers between devices  22.3 us (24%)
  Pallas kernels  11.5 us (12%)
  local copies, waits for them, and re-layouts  1.51 us (2%)
    all_to_all x1, blocking collectives, on_device(): lax.all_to_all(shares, ('z', 'x', 'core'), split_axis=0, concat_axis=0, t...  25.4 us
    all_to_all x1, starting transfers between devices, on_device(): lax.all_to_all(packed, ('z', 'x', 'core'), split_axis=0, concat_axis=0, t...  13 us
    all_to_all x1, waiting for transfers between devices, on_device(): lax.all_to_all(packed, ('z', 'x', 'core'), split_axis=0, concat_axis=0, t...  11.7 us
    pallas_call x4, Pallas kernels, call(): pl.pallas_call(kernel, out_shape=outs, in_specs=[pl.BlockSpec(memory_spac...  11.5 us
    all_to_all x1, starting transfers between devices, on_device(): lax.all_to_all(grads, ('z', 'y'), split_axis=0, concat_axis=0, tiled=True)  6.52 us
    ppermute x7, starting transfers between devices, on_device(): other = [lax.ppermute(block, 'core', [(0, 1), (1, 0)]) for block in own]  5.99 us
    ppermute x1, waiting for transfers between devices, on_device(): across_low = lax.ppermute(near_low, 'x', rings)  3.59 us
    ppermute x1, waiting for transfers between devices, on_device(): far_low = lax.ppermute(held[half:], 'x', rings)  3.55 us
  transfers between devices with their start and end apart: 15, of which 5 were waited for; matrix products, arithmetic and copies ran while one was open for 1% of the time, Pallas kernels for 3%

profile of v2, /device:TPU:1, one launch (start us, length us, event | category | flops | bytes accessed | tf_op | source)
XLA Modules:
  0.0 93.2 jit_solution(16337709723026938372)
XLA Ops:
  0.6 0.0 copy-start
  0.6 0.0 copy-start.1
  0.7 2.7 %pack.1 = bf16[64,24,128]{2,1,0:T(8,128)(2,1)} custom-call(bf16[256,128]{1,0:T(8,128)(2,1)} %key_in.1, bf16[256,128]{1,0:T(8,128)(2,1)} %value_in.1, bf16[256,128]{1,0:T(8,128)(2,1)} %grad_in.1, bf16[256,128]{1,0:T(8,128)(2,1)} %query_in.1, f32[256,128]{1,0:T(8,128)} %taps_in.1, bf16[512,512]{1,0:T(8,128)(2,1)} %constant.4.clone.order_in), custom_call_target="tpu_custom_call" | custom-call | tf_op jit(solution)/shard_map/pack/pallas_call | solution.py:270
  3.4 13.0 %all-to-all-start = ((bf16[64,24,128]{2,1,0:T(8,128)(2,1)}), bf16[64,24,128]{2,1,0:T(8,128)(2,1)S(1)}, u32[]{:S(2)}, u32[]{:S(2)}) async-start(bf16[64,24,128]{2,1,0:T(8,128)(2,1)} %pack.1), calls=%async_computation | async-start | bytes 786432 | tf_op jit(solution)/shard_map/all_to_all | solution.py:302
  16.4 0.0 copy-done.1
  16.4 0.7 fusion.1
  17.1 2.6 %collective-permute-start.1 = (bf16[128,1024]{1,0:T(8,128)(2,1)}, bf16[128,1024]{1,0:T(8,128)(2,1)S(1)}, u32[]{:S(2)}, u32[]{:S(2)}) collective-permute-start(bf16[128,1024]{1,0:T(8,128)(2,1)} %get-tuple-element.16), channel_id=1, source_target_pairs={{0,24},{24,0},{8,16},{16,8},{1,25},{25,1},{9,17},{17,9},{2,26},{26... | collective-permute-start | bytes 786440 | tf_op jit(solution)/shard_map/ppermute | solution.py:291
  19.7 0.0 collective-permute-start
  19.7 11.7 %all-to-all-done.got_ref = bf16[64,24,128]{2,1,0:T(8,128)(2,1)S(1)} async-done(((bf16[64,24,128]{2,1,0:T(8,128)(2,1)}), bf16[64,24,128]{2,1,0:T(8,128)(2,1)S(1)}, u32[]{:S(2)}, u32[]{:S(2)}) %all-to-all-start) | async-done | bytes 393248 | tf_op jit(solution)/shard_map/all_to_all | solution.py:302
  31.5 0.0 copy-done
  31.5 3.0 %conv.1 = (bf16[32,96,128]{2,1,0:T(8,128)(2,1)}, f32[64,8,128]{2,1,0:T(8,128)S(1)}) custom-call(bf16[64,24,128]{2,1,0:T(8,128)(2,1)S(1)} %all-to-all-done.got_ref, bf16[1344,512]{1,0:T(8,128)(2,1)S(1)} %copy-done), custom_call_target="tpu_custom_call" | custom-call | tf_op jit(solution)/shard_map/conv/pallas_call | solution.py:270
  34.5 0.0 collective-permute-done.1.rest_2_
  34.5 0.0 collective-permute-done.rest_1_
  34.5 6.5 %all-to-all-start.1 = ((bf16[32,96,128]{2,1,0:T(8,128)(2,1)}), bf16[32,96,128]{2,1,0:T(8,128)(2,1)}, u32[]{:S(2)}, u32[]{:S(2)}) async-start(bf16[32,96,128]{2,1,0:T(8,128)(2,1)} %get-tuple-element.9), calls=%async_computation.1 | async-start | bytes 1572864 | tf_op jit(solution)/shard_map/all_to_all | solution.py:324
  41.0 1.2 %collective-permute-start.6 = (bf16[256,1024]{1,0:T(8,128)(2,1)S(1)}, bf16[256,1024]{1,0:T(8,128)(2,1)S(1)}, u32[]{:S(2)}, u32[]{:S(2)}) collective-permute-start(bf16[256,1024]{1,0:T(8,128)(2,1)S(1)} %copy-done.1), channel_id=1, source_target_pairs={{0,4},{4,0},{1,5},{5,1},{2,6},{6,2},{3,7},{7,3},{8,12},{12,8},{9,1... | collective-permute-start | bytes 1572872 | tf_op jit(solution)/shard_map/ppermute | solution.py:323
  42.2 0.1 collective-permute-start.7
  42.3 1.0 %collective-permute-start.5 = (bf16[128,1024]{1,0:T(8,128)(2,1)S(1)}, bf16[128,1024]{1,0:T(8,128)(2,1)S(1)}, u32[]{:S(2)}, u32[]{:S(2)}) collective-permute-start(bf16[128,1024]{1,0:T(8,128)(2,1)S(1)} %collective-permute-done.rest_1_), channel_id=1, source_target_pairs={{0,24},{24,0},{8,16},{16,8},{1,25},{25,1},{9,17},{17,9},{2,26},{26... | collective-permute-start | bytes 786440 | tf_op jit(solution)/shard_map/ppermute | solution.py:321
  43.2 0.0 collective-permute-start.4
  43.3 1.8 %collective-permute-start.3 = (bf16[128,1024]{1,0:T(8,128)(2,1)S(1)}, bf16[128,1024]{1,0:T(8,128)(2,1)S(1)}, u32[]{:S(2)}, u32[]{:S(2)}) collective-permute-start(bf16[128,1024]{1,0:T(8,128)(2,1)S(1)} %get-tuple-element.14), channel_id=1, source_target_pairs={{0,24},{24,0},{8,16},{16,8},{1,25},{25,1},{9,17},{17,9},{2,26},{26... | collective-permute-start | bytes 786440 | tf_op jit(solution)/shard_map/ppermute | solution.py:319
  45.1 0.0 collective-permute-done.6.rest_7_
  45.1 0.0 copy-start.2
  45.1 0.9 collective-permute-start.2
  45.9 0.0 collective-permute-done.7.rest_8_
  45.9 0.0 copy-start.3
  45.9 1.5 %collective-permute-start.8 = (bf16[128,1024]{1,0:T(8,128)(2,1)S(1)}, bf16[128,1024]{1,0:T(8,128)(2,1)S(1)}, u32[]{:S(2)}, u32[]{:S(2)}) collective-permute-start(bf16[128,1024]{1,0:T(8,128)(2,1)S(1)} %collective-permute-done.1.rest_2_), channel_id=1, source_target_pairs={{0,4},{4,0},{1,5},{5,1},{2,6},{6,2},{3,7},{7,3},{8,12},{12,8},{9,1... | collective-permute-start | bytes 786440 | tf_op jit(solution)/shard_map/ppermute | solution.py:323
  47.5 3.6 %collective-permute-done.5.rest_6_ = bf16[128,1024]{1,0:T(8,128)(2,1)S(1)} collective-permute-done((bf16[128,1024]{1,0:T(8,128)(2,1)S(1)}, bf16[128,1024]{1,0:T(8,128)(2,1)S(1)}, u32[]{:S(2)}, u32[]{:S(2)}) %collective-permute-start.5) | collective-permute-done | bytes 262176 | tf_op jit(solution)/shard_map/ppermute | solution.py:321
  51.1 2.0 %collective-permute-start.12 = (bf16[128,1024]{1,0:T(8,128)(2,1)S(1)}, bf16[128,1024]{1,0:T(8,128)(2,1)S(1)}, u32[]{:S(2)}, u32[]{:S(2)}) collective-permute-start(bf16[128,1024]{1,0:T(8,128)(2,1)S(1)} %collective-permute-done.5.rest_6_), channel_id=1, source_target_pairs={{0,4},{4,0},{1,5},{5,1},{2,6},{6,2},{3,7},{7,3},{8,12},{12,8},{9,1... | collective-permute-start | bytes 786440 | tf_op jit(solution)/shard_map/ppermute | solution.py:323
  53.0 0.0 collective-permute-done.4.rest_5_
  53.1 0.1 collective-permute-start.11
  53.1 3.5 %collective-permute-done.3.rest_4_ = bf16[128,1024]{1,0:T(8,128)(2,1)S(1)} collective-permute-done((bf16[128,1024]{1,0:T(8,128)(2,1)S(1)}, bf16[128,1024]{1,0:T(8,128)(2,1)S(1)}, u32[]{:S(2)}, u32[]{:S(2)}) %collective-permute-start.3) | collective-permute-done | bytes 262176 | tf_op jit(solution)/shard_map/ppermute | solution.py:319
  56.7 1.1 %collective-permute-start.10 = (bf16[128,1024]{1,0:T(8,128)(2,1)S(1)}, bf16[128,1024]{1,0:T(8,128)(2,1)S(1)}, u32[]{:S(2)}, u32[]{:S(2)}) collective-permute-start(bf16[128,1024]{1,0:T(8,128)(2,1)S(1)} %collective-permute-done.3.rest_4_), channel_id=1, source_target_pairs={{0,4},{4,0},{1,5},{5,1},{2,6},{6,2},{3,7},{7,3},{8,12},{12,8},{9,1... | collective-permute-start | bytes 786440 | tf_op jit(solution)/shard_map/ppermute | solution.py:323
  57.8 0.0 collective-permute-done.2.rest_3_
  57.8 0.0 collective-permute-start.9
  57.8 0.0 collective-permute-done.8.rest_9_
  57.8 0.0 copy-start.4
  57.8 0.0 collective-permute-done.12.rest_13_
  57.9 0.0 copy-start.5
  57.9 0.0 collective-permute-done.11.rest_12_
  57.9 0.0 copy-start.6
  57.9 1.4 %collective-permute-done.10.rest_11_ = bf16[128,1024]{1,0:T(8,128)(2,1)S(1)} collective-permute-done((bf16[128,1024]{1,0:T(8,128)(2,1)S(1)}, bf16[128,1024]{1,0:T(8,128)(2,1)S(1)}, u32[]{:S(2)}, u32[]{:S(2)}) %collective-permute-start.10) | collective-permute-done | bytes 262176 | tf_op jit(solution)/shard_map/ppermute | solution.py:323
  59.3 0.0 copy-start.7
  59.3 0.7 copy-done.7
  60.0 0.0 collective-permute-done.9.rest_10_
  60.0 2.1 %all-to-all-done.1.got_ref = bf16[32,96,128]{2,1,0:T(8,128)(2,1)} async-done(((bf16[32,96,128]{2,1,0:T(8,128)(2,1)}), bf16[32,96,128]{2,1,0:T(8,128)(2,1)}, u32[]{:S(2)}, u32[]{:S(2)}) %all-to-all-start.1) | async-done | bytes 786464 | tf_op jit(solution)/shard_map/all_to_all | solution.py:324
  62.0 0.0 copy-done.2
  62.0 0.0 copy-done.3
  62.0 0.0 copy-done.4
  62.1 0.0 copy-done.5
  62.1 0.0 copy-done.6
  62.1 4.8 %share.1 = bf16[64,32,128]{2,1,0:T(8,128)(2,1)} custom-call(bf16[32,96,128]{2,1,0:T(8,128)(2,1)} %all-to-all-done.1.got_ref, f32[64,8,128]{2,1,0:T(8,128)S(1)} %get-tuple-element.10.lag_ref, bf16[256,1024]{1,0:T(8,128)(2,1)} %rest_0_.1, bf16[128,1024]{1,0:T(8,128)(2,1)S(1)} %collective-permute-done.rest_1_, ...), custom_call_target="tpu_custom_call" | custom-call | tf_op jit(solution)/shard_map/share/pallas_call | solution.py:270
  66.9 25.4 %all_to_all.15.got_ref = bf16[64,32,128]{2,1,0:T(8,128)(2,1)S(1)} all-to-all(bf16[64,32,128]{2,1,0:T(8,128)(2,1)} %share.1), channel_id=1, replica_groups=mesh['z'=8,'x'=4,'core'=2,'y'=4] {'z','x','core'}, dimensions={0} | all-to-all | bytes 1048576 | tf_op jit(solution)/shard_map/all_to_all | solution.py:339
  92.3 0.9 finish.1
  (1 shorter events, 0.0 us)
Async XLA Ops:
  0.6 30.8 %copy-start = (bf16[1344,512]{1,0:T(8,128)(2,1)S(1)}, bf16[1344,512]{1,0:T(8,128)(2,1)}, u32[]{:S(2)}) copy-start(bf16[1344,512]{1,0:T(8,128)(2,1)} %constant.5.clone.table_ref) | copy-start | bytes 4128772
  0.6 15.8 %copy-start.1 = (bf16[256,1024]{1,0:T(8,128)(2,1)S(1)}, bf16[256,1024]{1,0:T(8,128)(2,1)}, u32[]{:S(2)}) copy-start(bf16[256,1024]{1,0:T(8,128)(2,1)} %rest_0_.1) | copy-start | bytes 1572868
  3.4 28.1 %all-to-all-start = ((bf16[64,24,128]{2,1,0:T(8,128)(2,1)}), bf16[64,24,128]{2,1,0:T(8,128)(2,1)S(1)}, u32[]{:S(2)}, u32[]{:S(2)}) async-start(bf16[64,24,128]{2,1,0:T(8,128)(2,1)} %pack.1), calls=%async_computation | async-start | bytes 786432 | tf_op jit(solution)/shard_map/all_to_all | solution.py:302
  17.1 17.3 %collective-permute-start.1 = (bf16[128,1024]{1,0:T(8,128)(2,1)}, bf16[128,1024]{1,0:T(8,128)(2,1)S(1)}, u32[]{:S(2)}, u32[]{:S(2)}) collective-permute-start(bf16[128,1024]{1,0:T(8,128)(2,1)} %get-tuple-element.16), channel_id=1, source_target_pairs={{0,24},{24,0},{8,16},{16,8},{1,25},{25,1},{9,17},{17,9},{2,26},{26... | collective-permute-start | bytes 786440 | tf_op jit(solution)/shard_map/ppermute | solution.py:291
  19.7 14.7 %collective-permute-start = (bf16[128,1024]{1,0:T(8,128)(2,1)S(1)}, bf16[128,1024]{1,0:T(8,128)(2,1)S(1)}, u32[]{:S(2)}, u32[]{:S(2)}) collective-permute-start(bf16[128,1024]{1,0:T(8,128)(2,1)S(1)} %get-tuple-element.17), channel_id=1, source_target_pairs={{0,8},{8,0},{16,24},{24,16},{1,9},{9,1},{17,25},{25,17},{2,10},{10... | collective-permute-start | bytes 786440 | tf_op jit(solution)/shard_map/ppermute | solution.py:290
  34.5 27.6 %all-to-all-start.1 = ((bf16[32,96,128]{2,1,0:T(8,128)(2,1)}), bf16[32,96,128]{2,1,0:T(8,128)(2,1)}, u32[]{:S(2)}, u32[]{:S(2)}) async-start(bf16[32,96,128]{2,1,0:T(8,128)(2,1)} %get-tuple-element.9), calls=%async_computation.1 | async-start | bytes 1572864 | tf_op jit(solution)/shard_map/all_to_all | solution.py:324
  41.0 4.1 %collective-permute-start.6 = (bf16[256,1024]{1,0:T(8,128)(2,1)S(1)}, bf16[256,1024]{1,0:T(8,128)(2,1)S(1)}, u32[]{:S(2)}, u32[]{:S(2)}) collective-permute-start(bf16[256,1024]{1,0:T(8,128)(2,1)S(1)} %copy-done.1), channel_id=1, source_target_pairs={{0,4},{4,0},{1,5},{5,1},{2,6},{6,2},{3,7},{7,3},{8,12},{12,8},{9,1... | collective-permute-start | bytes 1572872 | tf_op jit(solution)/shard_map/ppermute | solution.py:323
  42.2 3.8 %collective-permute-start.7 = (bf16[128,1024]{1,0:T(8,128)(2,1)S(1)}, bf16[128,1024]{1,0:T(8,128)(2,1)S(1)}, u32[]{:S(2)}, u32[]{:S(2)}) collective-permute-start(bf16[128,1024]{1,0:T(8,128)(2,1)S(1)} %collective-permute-done.rest_1_), channel_id=1, source_target_pairs={{0,4},{4,0},{1,5},{5,1},{2,6},{6,2},{3,7},{7,3},{8,12},{12,8},{9,1... | collective-permute-start | bytes 786440 | tf_op jit(solution)/shard_map/ppermute | solution.py:323
  42.3 8.8 %collective-permute-start.5 = (bf16[128,1024]{1,0:T(8,128)(2,1)S(1)}, bf16[128,1024]{1,0:T(8,128)(2,1)S(1)}, u32[]{:S(2)}, u32[]{:S(2)}) collective-permute-start(bf16[128,1024]{1,0:T(8,128)(2,1)S(1)} %collective-permute-done.rest_1_), channel_id=1, source_target_pairs={{0,24},{24,0},{8,16},{16,8},{1,25},{25,1},{9,17},{17,9},{2,26},{26... | collective-permute-start | bytes 786440 | tf_op jit(solution)/shard_map/ppermute | solution.py:321
  43.2 9.8 %collective-permute-start.4 = (bf16[128,1024]{1,0:T(8,128)(2,1)S(1)}, bf16[128,1024]{1,0:T(8,128)(2,1)S(1)}, u32[]{:S(2)}, u32[]{:S(2)}) collective-permute-start(bf16[128,1024]{1,0:T(8,128)(2,1)S(1)} %collective-permute-done.1.rest_2_), channel_id=1, source_target_pairs={{0,8},{8,0},{16,24},{24,16},{1,9},{9,1},{17,25},{25,17},{2,10},{10... | collective-permute-start | bytes 786440 | tf_op jit(solution)/shard_map/ppermute | solution.py:320
  43.3 13.4 %collective-permute-start.3 = (bf16[128,1024]{1,0:T(8,128)(2,1)S(1)}, bf16[128,1024]{1,0:T(8,128)(2,1)S(1)}, u32[]{:S(2)}, u32[]{:S(2)}) collective-permute-start(bf16[128,1024]{1,0:T(8,128)(2,1)S(1)} %get-tuple-element.14), channel_id=1, source_target_pairs={{0,24},{24,0},{8,16},{16,8},{1,25},{25,1},{9,17},{17,9},{2,26},{26... | collective-permute-start | bytes 786440 | tf_op jit(solution)/shard_map/ppermute | solution.py:319
  45.1 17.0 %copy-start.2 = (bf16[256,1024]{1,0:T(8,128)(2,1)}, bf16[256,1024]{1,0:T(8,128)(2,1)S(1)}, u32[]{:S(2)}) copy-start(bf16[256,1024]{1,0:T(8,128)(2,1)S(1)} %collective-permute-done.6.rest_7_) | copy-start | bytes 1572868
  45.1 12.7 %collective-permute-start.2 = (bf16[128,1024]{1,0:T(8,128)(2,1)S(1)}, bf16[128,1024]{1,0:T(8,128)(2,1)S(1)}, u32[]{:S(2)}, u32[]{:S(2)}) collective-permute-start(bf16[128,1024]{1,0:T(8,128)(2,1)S(1)} %get-tuple-element.15), channel_id=1, source_target_pairs={{0,8},{8,0},{16,24},{24,16},{1,9},{9,1},{17,25},{25,17},{2,10},{10... | collective-permute-start | bytes 786440 | tf_op jit(solution)/shard_map/ppermute | solution.py:318
  45.9 16.1 %copy-start.3 = (bf16[128,1024]{1,0:T(8,128)(2,1)}, bf16[128,1024]{1,0:T(8,128)(2,1)S(1)}, u32[]{:S(2)}) copy-start(bf16[128,1024]{1,0:T(8,128)(2,1)S(1)} %collective-permute-done.7.rest_8_) | copy-start | bytes 786436
  45.9 11.9 %collective-permute-start.8 = (bf16[128,1024]{1,0:T(8,128)(2,1)S(1)}, bf16[128,1024]{1,0:T(8,128)(2,1)S(1)}, u32[]{:S(2)}, u32[]{:S(2)}) collective-permute-start(bf16[128,1024]{1,0:T(8,128)(2,1)S(1)} %collective-permute-done.1.rest_2_), channel_id=1, source_target_pairs={{0,4},{4,0},{1,5},{5,1},{2,6},{6,2},{3,7},{7,3},{8,12},{12,8},{9,1... | collective-permute-start | bytes 786440 | tf_op jit(solution)/shard_map/ppermute | solution.py:323
  51.1 6.8 %collective-permute-start.12 = (bf16[128,1024]{1,0:T(8,128)(2,1)S(1)}, bf16[128,1024]{1,0:T(8,128)(2,1)S(1)}, u32[]{:S(2)}, u32[]{:S(2)}) collective-permute-start(bf16[128,1024]{1,0:T(8,128)(2,1)S(1)} %collective-permute-done.5.rest_6_), channel_id=1, source_target_pairs={{0,4},{4,0},{1,5},{5,1},{2,6},{6,2},{3,7},{7,3},{8,12},{12,8},{9,1... | collective-permute-start | bytes 786440 | tf_op jit(solution)/shard_map/ppermute | solution.py:323
  53.1 4.8 %collective-permute-start.11 = (bf16[128,1024]{1,0:T(8,128)(2,1)S(1)}, bf16[128,1024]{1,0:T(8,128)(2,1)S(1)}, u32[]{:S(2)}, u32[]{:S(2)}) collective-permute-start(bf16[128,1024]{1,0:T(8,128)(2,1)S(1)} %collective-permute-done.4.rest_5_), channel_id=1, source_target_pairs={{0,4},{4,0},{1,5},{5,1},{2,6},{6,2},{3,7},{7,3},{8,12},{12,8},{9,1... | collective-permute-start | bytes 786440 | tf_op jit(solution)/shard_map/ppermute | solution.py:323
  56.7 2.6 %collective-permute-start.10 = (bf16[128,1024]{1,0:T(8,128)(2,1)S(1)}, bf16[128,1024]{1,0:T(8,128)(2,1)S(1)}, u32[]{:S(2)}, u32[]{:S(2)}) collective-permute-start(bf16[128,1024]{1,0:T(8,128)(2,1)S(1)} %collective-permute-done.3.rest_4_), channel_id=1, source_target_pairs={{0,4},{4,0},{1,5},{5,1},{2,6},{6,2},{3,7},{7,3},{8,12},{12,8},{9,1... | collective-permute-start | bytes 786440 | tf_op jit(solution)/shard_map/ppermute | solution.py:323
  57.8 2.2 %collective-permute-start.9 = (bf16[128,1024]{1,0:T(8,128)(2,1)S(1)}, bf16[128,1024]{1,0:T(8,128)(2,1)}, u32[]{:S(2)}, u32[]{:S(2)}) collective-permute-start(bf16[128,1024]{1,0:T(8,128)(2,1)S(1)} %collective-permute-done.2.rest_3_), channel_id=1, source_target_pairs={{0,4},{4,0},{1,5},{5,1},{2,6},{6,2},{3,7},{7,3},{8,12},{12,8},{9,1... | collective-permute-start | bytes 786440 | tf_op jit(solution)/shard_map/ppermute | solution.py:323
  57.8 4.2 %copy-start.4 = (bf16[128,1024]{1,0:T(8,128)(2,1)}, bf16[128,1024]{1,0:T(8,128)(2,1)S(1)}, u32[]{:S(2)}) copy-start(bf16[128,1024]{1,0:T(8,128)(2,1)S(1)} %collective-permute-done.8.rest_9_) | copy-start | bytes 786436
  57.9 4.2 %copy-start.5 = (bf16[128,1024]{1,0:T(8,128)(2,1)}, bf16[128,1024]{1,0:T(8,128)(2,1)S(1)}, u32[]{:S(2)}) copy-start(bf16[128,1024]{1,0:T(8,128)(2,1)S(1)} %collective-permute-done.12.rest_13_) | copy-start | bytes 786436
  57.9 4.2 %copy-start.6 = (bf16[128,1024]{1,0:T(8,128)(2,1)}, bf16[128,1024]{1,0:T(8,128)(2,1)S(1)}, u32[]{:S(2)}) copy-start(bf16[128,1024]{1,0:T(8,128)(2,1)S(1)} %collective-permute-done.11.rest_12_) | copy-start | bytes 786436
  59.3 0.7 copy-start.7

commit v3 on v2

--- a/solution.py
+++ b/solution.py
@@ -187,8 +187,8 @@
     lag_ref[...] = lag_rows_ref[...].reshape(BLOCKS, 8, 128)
 
 
-def share_kernel(got_ref, lag_ref, *rest):
-    inputs, (out_ref, rows_ref, held_ref, sums_ref, done) = rest[:14], rest[14:]
+def share_kernel(got_in, lag_in, *rest):
+    inputs, (out_ref, got_ref, lag_ref, rows_ref, held_ref, sums_ref, done) = rest[:14], rest[14:]
     x, core = lax.axis_index("x"), lax.axis_index("core")
     across = lax.rem(x + 2, NX)
     beside = x + 1 - 2 * lax.rem(x, 2)
@@ -210,7 +210,8 @@
         ):
             start = pl.multiple_of((NCORE * place + unit) * BLOCK_LEN + offset, half)
             pairs.append((source, held_ref.at[pl.ds(start, length)]))
-    copies = fetch(pairs, done)
+    copies = fetch([(got_in, got_ref), (lag_in, lag_ref), *pairs], done)
+    copies[0].wait()
     rows_ref[...] = got_ref[...].astype(f32).reshape(32 * 96, 128)
     left = []
     for a in range(NA):
@@ -230,7 +231,7 @@
                     )
         left.append(jnp.concatenate(tiles, axis=0).astype(bf16))
     left = jnp.concatenate(left, axis=1)
-    for copy in copies:
+    for copy in copies[1:]:
         copy.wait()
     total = product(left, held_ref[...], ((1,), (0,)))
     for lane in range(8):
@@ -326,13 +327,15 @@
         share_kernel,
         "share",
         (stacked, lags, *own, *other),
-        [VMEM, VMEM] + [pl.ANY] * 14,
+        [pl.ANY] * 16,
         jax.ShapeDtypeStruct((BLOCKS, 32, 128), bf16),
         [
+            VMEM((32, 96, 128), bf16),
+            VMEM((BLOCKS, 8, 128), f32),
             VMEM((32 * 96, 128), f32),
             VMEM((2048, 1024), bf16),
             VMEM((1536, 128), f32),
-            pltpu.SemaphoreType.DMA((14,)),
+            pltpu.SemaphoreType.DMA((16,)),
         ],
         52,
     )

time: 93.6 us -> 92.8 us (level)
  no operation moved by 1% of the time
where the time goes in v3:
time: 92.8 us; the launch traced here: 92.5 us
  starting transfers between devices  31.7 us (34%)
  blocking collectives  25.4 us (27%)
  waiting for transfers between devices  22.3 us (24%)
  Pallas kernels  10.8 us (12%)
  local copies, waits for them, and re-layouts  1.51 us (2%)
    all_to_all x1, blocking collectives, on_device(): lax.all_to_all(shares, ('z', 'x', 'core'), split_axis=0, concat_axis=0, t...  25.4 us
    all_to_all x1, starting transfers between devices, on_device(): lax.all_to_all(packed, ('z', 'x', 'core'), split_axis=0, concat_axis=0, t...  13 us
    all_to_all x1, waiting for transfers between devices, on_device(): lax.all_to_all(packed, ('z', 'x', 'core'), split_axis=0, concat_axis=0, t...  11.7 us
    pallas_call x4, Pallas kernels, call(): pl.pallas_call(kernel, out_shape=outs, in_specs=[pl.BlockSpec(memory_spac...  10.8 us
    all_to_all x1, starting transfers between devices, on_device(): lax.all_to_all(grads, ('z', 'y'), split_axis=0, concat_axis=0, tiled=True)  6.52 us
    ppermute x7, starting transfers between devices, on_device(): other = [lax.ppermute(block, 'core', [(0, 1), (1, 0)]) for block in own]  5.99 us
    ppermute x1, waiting for transfers between devices, on_device(): across_low = lax.ppermute(near_low, 'x', rings)  3.59 us
    ppermute x1, waiting for transfers between devices, on_device(): far_low = lax.ppermute(held[half:], 'x', rings)  3.55 us
  transfers between devices with their start and end apart: 15, of which 5 were waited for; matrix products, arithmetic and copies ran while one was open for 1% of the time, Pallas kernels for 3%

profile of v3, /device:TPU:1, one launch (start us, length us, event | category | flops | bytes accessed | tf_op | source)
XLA Modules:
  0.0 92.5 jit_solution(11885555195648287024)
XLA Ops:
  0.6 0.0 copy-start
  0.6 0.0 copy-start.1
  0.7 2.7 %pack.1 = bf16[64,24,128]{2,1,0:T(8,128)(2,1)} custom-call(bf16[256,128]{1,0:T(8,128)(2,1)} %key_in.1, bf16[256,128]{1,0:T(8,128)(2,1)} %value_in.1, bf16[256,128]{1,0:T(8,128)(2,1)} %grad_in.1, bf16[256,128]{1,0:T(8,128)(2,1)} %query_in.1, f32[256,128]{1,0:T(8,128)} %taps_in.1, bf16[512,512]{1,0:T(8,128)(2,1)} %constant.4.clone.order_in), custom_call_target="tpu_custom_call" | custom-call | tf_op jit(solution)/shard_map/pack/pallas_call | solution.py:271
  3.4 13.0 %all-to-all-start = ((bf16[64,24,128]{2,1,0:T(8,128)(2,1)}), bf16[64,24,128]{2,1,0:T(8,128)(2,1)S(1)}, u32[]{:S(2)}, u32[]{:S(2)}) async-start(bf16[64,24,128]{2,1,0:T(8,128)(2,1)} %pack.1), calls=%async_computation | async-start | bytes 786432 | tf_op jit(solution)/shard_map/all_to_all | solution.py:303
  16.4 0.0 copy-done.1
  16.4 0.7 fusion.1
  17.1 2.6 %collective-permute-start.1 = (bf16[128,1024]{1,0:T(8,128)(2,1)}, bf16[128,1024]{1,0:T(8,128)(2,1)S(1)}, u32[]{:S(2)}, u32[]{:S(2)}) collective-permute-start(bf16[128,1024]{1,0:T(8,128)(2,1)} %get-tuple-element.16), channel_id=1, source_target_pairs={{0,24},{24,0},{8,16},{16,8},{1,25},{25,1},{9,17},{17,9},{2,26},{26... | collective-permute-start | bytes 786440 | tf_op jit(solution)/shard_map/ppermute | solution.py:292
  19.7 0.0 collective-permute-start
  19.7 11.7 %all-to-all-done.got_ref = bf16[64,24,128]{2,1,0:T(8,128)(2,1)S(1)} async-done(((bf16[64,24,128]{2,1,0:T(8,128)(2,1)}), bf16[64,24,128]{2,1,0:T(8,128)(2,1)S(1)}, u32[]{:S(2)}, u32[]{:S(2)}) %all-to-all-start) | async-done | bytes 393248 | tf_op jit(solution)/shard_map/all_to_all | solution.py:303
  31.5 0.0 copy-done
  31.5 3.0 %conv.1 = (bf16[32,96,128]{2,1,0:T(8,128)(2,1)}, f32[64,8,128]{2,1,0:T(8,128)S(1)}) custom-call(bf16[64,24,128]{2,1,0:T(8,128)(2,1)S(1)} %all-to-all-done.got_ref, bf16[1344,512]{1,0:T(8,128)(2,1)S(1)} %copy-done), custom_call_target="tpu_custom_call" | custom-call | tf_op jit(solution)/shard_map/conv/pallas_call | solution.py:271
  34.5 0.0 collective-permute-done.1.rest_2_
  34.5 0.0 collective-permute-done.rest_1_
  34.5 6.5 %all-to-all-start.1 = ((bf16[32,96,128]{2,1,0:T(8,128)(2,1)}), bf16[32,96,128]{2,1,0:T(8,128)(2,1)}, u32[]{:S(2)}, u32[]{:S(2)}) async-start(bf16[32,96,128]{2,1,0:T(8,128)(2,1)} %get-tuple-element.9), calls=%async_computation.1 | async-start | bytes 1572864 | tf_op jit(solution)/shard_map/all_to_all | solution.py:325
  41.0 1.2 %collective-permute-start.6 = (bf16[256,1024]{1,0:T(8,128)(2,1)S(1)}, bf16[256,1024]{1,0:T(8,128)(2,1)S(1)}, u32[]{:S(2)}, u32[]{:S(2)}) collective-permute-start(bf16[256,1024]{1,0:T(8,128)(2,1)S(1)} %copy-done.1), channel_id=1, source_target_pairs={{0,4},{4,0},{1,5},{5,1},{2,6},{6,2},{3,7},{7,3},{8,12},{12,8},{9,1... | collective-permute-start | bytes 1572872 | tf_op jit(solution)/shard_map/ppermute | solution.py:324
  42.2 0.1 collective-permute-start.7
  42.3 1.0 %collective-permute-start.5 = (bf16[128,1024]{1,0:T(8,128)(2,1)S(1)}, bf16[128,1024]{1,0:T(8,128)(2,1)S(1)}, u32[]{:S(2)}, u32[]{:S(2)}) collective-permute-start(bf16[128,1024]{1,0:T(8,128)(2,1)S(1)} %collective-permute-done.rest_1_), channel_id=1, source_target_pairs={{0,24},{24,0},{8,16},{16,8},{1,25},{25,1},{9,17},{17,9},{2,26},{26... | collective-permute-start | bytes 786440 | tf_op jit(solution)/shard_map/ppermute | solution.py:322
  43.2 0.0 collective-permute-start.4
  43.3 1.8 %collective-permute-start.3 = (bf16[128,1024]{1,0:T(8,128)(2,1)S(1)}, bf16[128,1024]{1,0:T(8,128)(2,1)S(1)}, u32[]{:S(2)}, u32[]{:S(2)}) collective-permute-start(bf16[128,1024]{1,0:T(8,128)(2,1)S(1)} %get-tuple-element.14), channel_id=1, source_target_pairs={{0,24},{24,0},{8,16},{16,8},{1,25},{25,1},{9,17},{17,9},{2,26},{26... | collective-permute-start | bytes 786440 | tf_op jit(solution)/shard_map/ppermute | solution.py:320
  45.1 0.0 collective-permute-done.6.rest_7_
  45.1 0.0 copy-start.2
  45.1 0.9 collective-permute-start.2
  45.9 0.0 collective-permute-done.7.rest_8_
  45.9 0.0 copy-start.3
  45.9 1.5 %collective-permute-start.8 = (bf16[128,1024]{1,0:T(8,128)(2,1)S(1)}, bf16[128,1024]{1,0:T(8,128)(2,1)S(1)}, u32[]{:S(2)}, u32[]{:S(2)}) collective-permute-start(bf16[128,1024]{1,0:T(8,128)(2,1)S(1)} %collective-permute-done.1.rest_2_), channel_id=1, source_target_pairs={{0,4},{4,0},{1,5},{5,1},{2,6},{6,2},{3,7},{7,3},{8,12},{12,8},{9,1... | collective-permute-start | bytes 786440 | tf_op jit(solution)/shard_map/ppermute | solution.py:324
  47.5 3.6 %collective-permute-done.5.rest_6_ = bf16[128,1024]{1,0:T(8,128)(2,1)S(1)} collective-permute-done((bf16[128,1024]{1,0:T(8,128)(2,1)S(1)}, bf16[128,1024]{1,0:T(8,128)(2,1)S(1)}, u32[]{:S(2)}, u32[]{:S(2)}) %collective-permute-start.5) | collective-permute-done | bytes 262176 | tf_op jit(solution)/shard_map/ppermute | solution.py:322
  51.1 2.0 %collective-permute-start.12 = (bf16[128,1024]{1,0:T(8,128)(2,1)S(1)}, bf16[128,1024]{1,0:T(8,128)(2,1)S(1)}, u32[]{:S(2)}, u32[]{:S(2)}) collective-permute-start(bf16[128,1024]{1,0:T(8,128)(2,1)S(1)} %collective-permute-done.5.rest_6_), channel_id=1, source_target_pairs={{0,4},{4,0},{1,5},{5,1},{2,6},{6,2},{3,7},{7,3},{8,12},{12,8},{9,1... | collective-permute-start | bytes 786440 | tf_op jit(solution)/shard_map/ppermute | solution.py:324
  53.0 0.0 collective-permute-done.4.rest_5_
  53.1 0.1 collective-permute-start.11
  53.1 3.5 %collective-permute-done.3.rest_4_ = bf16[128,1024]{1,0:T(8,128)(2,1)S(1)} collective-permute-done((bf16[128,1024]{1,0:T(8,128)(2,1)S(1)}, bf16[128,1024]{1,0:T(8,128)(2,1)S(1)}, u32[]{:S(2)}, u32[]{:S(2)}) %collective-permute-start.3) | collective-permute-done | bytes 262176 | tf_op jit(solution)/shard_map/ppermute | solution.py:320
  56.7 1.1 %collective-permute-start.10 = (bf16[128,1024]{1,0:T(8,128)(2,1)S(1)}, bf16[128,1024]{1,0:T(8,128)(2,1)S(1)}, u32[]{:S(2)}, u32[]{:S(2)}) collective-permute-start(bf16[128,1024]{1,0:T(8,128)(2,1)S(1)} %collective-permute-done.3.rest_4_), channel_id=1, source_target_pairs={{0,4},{4,0},{1,5},{5,1},{2,6},{6,2},{3,7},{7,3},{8,12},{12,8},{9,1... | collective-permute-start | bytes 786440 | tf_op jit(solution)/shard_map/ppermute | solution.py:324
  57.8 0.0 collective-permute-done.2.rest_3_
  57.8 0.0 collective-permute-start.9
  57.8 0.0 collective-permute-done.8.rest_9_
  57.8 0.0 copy-start.4
  57.8 0.0 collective-permute-done.12.rest_13_
  57.9 0.0 copy-start.5
  57.9 0.0 collective-permute-done.11.rest_12_
  57.9 0.0 copy-start.6
  57.9 1.4 %collective-permute-done.10.rest_11_ = bf16[128,1024]{1,0:T(8,128)(2,1)S(1)} collective-permute-done((bf16[128,1024]{1,0:T(8,128)(2,1)S(1)}, bf16[128,1024]{1,0:T(8,128)(2,1)S(1)}, u32[]{:S(2)}, u32[]{:S(2)}) %collective-permute-start.10) | collective-permute-done | bytes 262176 | tf_op jit(solution)/shard_map/ppermute | solution.py:324
  59.3 0.0 copy-start.7
  59.3 0.7 copy-done.7
  60.0 0.0 collective-permute-done.9.rest_10_
  60.0 2.1 %all-to-all-done.1.got_in = bf16[32,96,128]{2,1,0:T(8,128)(2,1)} async-done(((bf16[32,96,128]{2,1,0:T(8,128)(2,1)}), bf16[32,96,128]{2,1,0:T(8,128)(2,1)}, u32[]{:S(2)}, u32[]{:S(2)}) %all-to-all-start.1) | async-done | bytes 786464 | tf_op jit(solution)/shard_map/all_to_all | solution.py:325
  62.0 0.0 copy-done.2
  62.0 0.0 copy-done.3
  62.0 0.0 copy-done.4
  62.1 0.0 copy-done.5
  62.1 0.0 copy-done.6
  62.1 4.1 %share.1 = bf16[64,32,128]{2,1,0:T(8,128)(2,1)} custom-call(bf16[32,96,128]{2,1,0:T(8,128)(2,1)} %all-to-all-done.1.got_in, f32[64,8,128]{2,1,0:T(8,128)S(1)} %get-tuple-element.10.lag_in, bf16[256,1024]{1,0:T(8,128)(2,1)} %rest_0_.1, bf16[128,1024]{1,0:T(8,128)(2,1)S(1)} %collective-permute-done.rest_1_, ...), custom_call_target="tpu_custom_call" | custom-call | tf_op jit(solution)/shard_map/share/pallas_call | solution.py:271
  66.2 25.4 %all_to_all.15.got_ref = bf16[64,32,128]{2,1,0:T(8,128)(2,1)S(1)} all-to-all(bf16[64,32,128]{2,1,0:T(8,128)(2,1)} %share.1), channel_id=1, replica_groups=mesh['z'=8,'x'=4,'core'=2,'y'=4] {'z','x','core'}, dimensions={0} | all-to-all | bytes 1048576 | tf_op jit(solution)/shard_map/all_to_all | solution.py:342
  91.6 0.9 finish.1
  (1 shorter events, 0.0 us)
Async XLA Ops:
  0.6 30.8 %copy-start = (bf16[1344,512]{1,0:T(8,128)(2,1)S(1)}, bf16[1344,512]{1,0:T(8,128)(2,1)}, u32[]{:S(2)}) copy-start(bf16[1344,512]{1,0:T(8,128)(2,1)} %constant.5.clone.table_ref) | copy-start | bytes 4128772
  0.6 15.8 %copy-start.1 = (bf16[256,1024]{1,0:T(8,128)(2,1)S(1)}, bf16[256,1024]{1,0:T(8,128)(2,1)}, u32[]{:S(2)}) copy-start(bf16[256,1024]{1,0:T(8,128)(2,1)} %rest_0_.1) | copy-start | bytes 1572868
  3.4 28.1 %all-to-all-start = ((bf16[64,24,128]{2,1,0:T(8,128)(2,1)}), bf16[64,24,128]{2,1,0:T(8,128)(2,1)S(1)}, u32[]{:S(2)}, u32[]{:S(2)}) async-start(bf16[64,24,128]{2,1,0:T(8,128)(2,1)} %pack.1), calls=%async_computation | async-start | bytes 786432 | tf_op jit(solution)/shard_map/all_to_all | solution.py:303
  17.1 17.3 %collective-permute-start.1 = (bf16[128,1024]{1,0:T(8,128)(2,1)}, bf16[128,1024]{1,0:T(8,128)(2,1)S(1)}, u32[]{:S(2)}, u32[]{:S(2)}) collective-permute-start(bf16[128,1024]{1,0:T(8,128)(2,1)} %get-tuple-element.16), channel_id=1, source_target_pairs={{0,24},{24,0},{8,16},{16,8},{1,25},{25,1},{9,17},{17,9},{2,26},{26... | collective-permute-start | bytes 786440 | tf_op jit(solution)/shard_map/ppermute | solution.py:292
  19.7 14.7 %collective-permute-start = (bf16[128,1024]{1,0:T(8,128)(2,1)S(1)}, bf16[128,1024]{1,0:T(8,128)(2,1)S(1)}, u32[]{:S(2)}, u32[]{:S(2)}) collective-permute-start(bf16[128,1024]{1,0:T(8,128)(2,1)S(1)} %get-tuple-element.17), channel_id=1, source_target_pairs={{0,8},{8,0},{16,24},{24,16},{1,9},{9,1},{17,25},{25,17},{2,10},{10... | collective-permute-start | bytes 786440 | tf_op jit(solution)/shard_map/ppermute | solution.py:291
  34.5 27.6 %all-to-all-start.1 = ((bf16[32,96,128]{2,1,0:T(8,128)(2,1)}), bf16[32,96,128]{2,1,0:T(8,128)(2,1)}, u32[]{:S(2)}, u32[]{:S(2)}) async-start(bf16[32,96,128]{2,1,0:T(8,128)(2,1)} %get-tuple-element.9), calls=%async_computation.1 | async-start | bytes 1572864 | tf_op jit(solution)/shard_map/all_to_all | solution.py:325
  41.0 4.1 %collective-permute-start.6 = (bf16[256,1024]{1,0:T(8,128)(2,1)S(1)}, bf16[256,1024]{1,0:T(8,128)(2,1)S(1)}, u32[]{:S(2)}, u32[]{:S(2)}) collective-permute-start(bf16[256,1024]{1,0:T(8,128)(2,1)S(1)} %copy-done.1), channel_id=1, source_target_pairs={{0,4},{4,0},{1,5},{5,1},{2,6},{6,2},{3,7},{7,3},{8,12},{12,8},{9,1... | collective-permute-start | bytes 1572872 | tf_op jit(solution)/shard_map/ppermute | solution.py:324
  42.2 3.8 %collective-permute-start.7 = (bf16[128,1024]{1,0:T(8,128)(2,1)S(1)}, bf16[128,1024]{1,0:T(8,128)(2,1)S(1)}, u32[]{:S(2)}, u32[]{:S(2)}) collective-permute-start(bf16[128,1024]{1,0:T(8,128)(2,1)S(1)} %collective-permute-done.rest_1_), channel_id=1, source_target_pairs={{0,4},{4,0},{1,5},{5,1},{2,6},{6,2},{3,7},{7,3},{8,12},{12,8},{9,1... | collective-permute-start | bytes 786440 | tf_op jit(solution)/shard_map/ppermute | solution.py:324
  42.3 8.8 %collective-permute-start.5 = (bf16[128,1024]{1,0:T(8,128)(2,1)S(1)}, bf16[128,1024]{1,0:T(8,128)(2,1)S(1)}, u32[]{:S(2)}, u32[]{:S(2)}) collective-permute-start(bf16[128,1024]{1,0:T(8,128)(2,1)S(1)} %collective-permute-done.rest_1_), channel_id=1, source_target_pairs={{0,24},{24,0},{8,16},{16,8},{1,25},{25,1},{9,17},{17,9},{2,26},{26... | collective-permute-start | bytes 786440 | tf_op jit(solution)/shard_map/ppermute | solution.py:322
  43.2 9.8 %collective-permute-start.4 = (bf16[128,1024]{1,0:T(8,128)(2,1)S(1)}, bf16[128,1024]{1,0:T(8,128)(2,1)S(1)}, u32[]{:S(2)}, u32[]{:S(2)}) collective-permute-start(bf16[128,1024]{1,0:T(8,128)(2,1)S(1)} %collective-permute-done.1.rest_2_), channel_id=1, source_target_pairs={{0,8},{8,0},{16,24},{24,16},{1,9},{9,1},{17,25},{25,17},{2,10},{10... | collective-permute-start | bytes 786440 | tf_op jit(solution)/shard_map/ppermute | solution.py:321
  43.3 13.4 %collective-permute-start.3 = (bf16[128,1024]{1,0:T(8,128)(2,1)S(1)}, bf16[128,1024]{1,0:T(8,128)(2,1)S(1)}, u32[]{:S(2)}, u32[]{:S(2)}) collective-permute-start(bf16[128,1024]{1,0:T(8,128)(2,1)S(1)} %get-tuple-element.14), channel_id=1, source_target_pairs={{0,24},{24,0},{8,16},{16,8},{1,25},{25,1},{9,17},{17,9},{2,26},{26... | collective-permute-start | bytes 786440 | tf_op jit(solution)/shard_map/ppermute | solution.py:320
  45.1 17.0 %copy-start.2 = (bf16[256,1024]{1,0:T(8,128)(2,1)}, bf16[256,1024]{1,0:T(8,128)(2,1)S(1)}, u32[]{:S(2)}) copy-start(bf16[256,1024]{1,0:T(8,128)(2,1)S(1)} %collective-permute-done.6.rest_7_) | copy-start | bytes 1572868
  45.1 12.7 %collective-permute-start.2 = (bf16[128,1024]{1,0:T(8,128)(2,1)S(1)}, bf16[128,1024]{1,0:T(8,128)(2,1)S(1)}, u32[]{:S(2)}, u32[]{:S(2)}) collective-permute-start(bf16[128,1024]{1,0:T(8,128)(2,1)S(1)} %get-tuple-element.15), channel_id=1, source_target_pairs={{0,8},{8,0},{16,24},{24,16},{1,9},{9,1},{17,25},{25,17},{2,10},{10... | collective-permute-start | bytes 786440 | tf_op jit(solution)/shard_map/ppermute | solution.py:319
  45.9 16.1 %copy-start.3 = (bf16[128,1024]{1,0:T(8,128)(2,1)}, bf16[128,1024]{1,0:T(8,128)(2,1)S(1)}, u32[]{:S(2)}) copy-start(bf16[128,1024]{1,0:T(8,128)(2,1)S(1)} %collective-permute-done.7.rest_8_) | copy-start | bytes 786436
  45.9 11.9 %collective-permute-start.8 = (bf16[128,1024]{1,0:T(8,128)(2,1)S(1)}, bf16[128,1024]{1,0:T(8,128)(2,1)S(1)}, u32[]{:S(2)}, u32[]{:S(2)}) collective-permute-start(bf16[128,1024]{1,0:T(8,128)(2,1)S(1)} %collective-permute-done.1.rest_2_), channel_id=1, source_target_pairs={{0,4},{4,0},{1,5},{5,1},{2,6},{6,2},{3,7},{7,3},{8,12},{12,8},{9,1... | collective-permute-start | bytes 786440 | tf_op jit(solution)/shard_map/ppermute | solution.py:324
  51.1 6.8 %collective-permute-start.12 = (bf16[128,1024]{1,0:T(8,128)(2,1)S(1)}, bf16[128,1024]{1,0:T(8,128)(2,1)S(1)}, u32[]{:S(2)}, u32[]{:S(2)}) collective-permute-start(bf16[128,1024]{1,0:T(8,128)(2,1)S(1)} %collective-permute-done.5.rest_6_), channel_id=1, source_target_pairs={{0,4},{4,0},{1,5},{5,1},{2,6},{6,2},{3,7},{7,3},{8,12},{12,8},{9,1... | collective-permute-start | bytes 786440 | tf_op jit(solution)/shard_map/ppermute | solution.py:324
  53.1 4.8 %collective-permute-start.11 = (bf16[128,1024]{1,0:T(8,128)(2,1)S(1)}, bf16[128,1024]{1,0:T(8,128)(2,1)S(1)}, u32[]{:S(2)}, u32[]{:S(2)}) collective-permute-start(bf16[128,1024]{1,0:T(8,128)(2,1)S(1)} %collective-permute-done.4.rest_5_), channel_id=1, source_target_pairs={{0,4},{4,0},{1,5},{5,1},{2,6},{6,2},{3,7},{7,3},{8,12},{12,8},{9,1... | collective-permute-start | bytes 786440 | tf_op jit(solution)/shard_map/ppermute | solution.py:324
  56.7 2.6 %collective-permute-start.10 = (bf16[128,1024]{1,0:T(8,128)(2,1)S(1)}, bf16[128,1024]{1,0:T(8,128)(2,1)S(1)}, u32[]{:S(2)}, u32[]{:S(2)}) collective-permute-start(bf16[128,1024]{1,0:T(8,128)(2,1)S(1)} %collective-permute-done.3.rest_4_), channel_id=1, source_target_pairs={{0,4},{4,0},{1,5},{5,1},{2,6},{6,2},{3,7},{7,3},{8,12},{12,8},{9,1... | collective-permute-start | bytes 786440 | tf_op jit(solution)/shard_map/ppermute | solution.py:324
  57.8 2.2 %collective-permute-start.9 = (bf16[128,1024]{1,0:T(8,128)(2,1)S(1)}, bf16[128,1024]{1,0:T(8,128)(2,1)}, u32[]{:S(2)}, u32[]{:S(2)}) collective-permute-start(bf16[128,1024]{1,0:T(8,128)(2,1)S(1)} %collective-permute-done.2.rest_3_), channel_id=1, source_target_pairs={{0,4},{4,0},{1,5},{5,1},{2,6},{6,2},{3,7},{7,3},{8,12},{12,8},{9,1... | collective-permute-start | bytes 786440 | tf_op jit(solution)/shard_map/ppermute | solution.py:324
  57.8 4.2 %copy-start.4 = (bf16[128,1024]{1,0:T(8,128)(2,1)}, bf16[128,1024]{1,0:T(8,128)(2,1)S(1)}, u32[]{:S(2)}) copy-start(bf16[128,1024]{1,0:T(8,128)(2,1)S(1)} %collective-permute-done.8.rest_9_) | copy-start | bytes 786436
  57.9 4.2 %copy-start.5 = (bf16[128,1024]{1,0:T(8,128)(2,1)}, bf16[128,1024]{1,0:T(8,128)(2,1)S(1)}, u32[]{:S(2)}) copy-start(bf16[128,1024]{1,0:T(8,128)(2,1)S(1)} %collective-permute-done.12.rest_13_) | copy-start | bytes 786436
  57.9 4.2 %copy-start.6 = (bf16[128,1024]{1,0:T(8,128)(2,1)}, bf16[128,1024]{1,0:T(8,128)(2,1)S(1)}, u32[]{:S(2)}) copy-start(bf16[128,1024]{1,0:T(8,128)(2,1)S(1)} %collective-permute-done.11.rest_12_) | copy-start | bytes 786436
  59.3 0.7 copy-start.7

commit v4 on v3

--- a/solution.py
+++ b/solution.py
@@ -20,14 +20,11 @@
 
 
 def pack_order():
-    order = np.zeros((8 * BLOCKS, 4 * SHARD_CH), np.float32)
-    for i in range(BLOCKS):
-        for s in range(2):
-            for j in range(2):
-                for half in range(2):
-                    row = i * 8 + 4 * s + 2 * j + half
-                    order[row, (2 * s + half) * SHARD_CH + 64 * j + i] = 1.0
-    return order.astype(jnp.bfloat16)
+    rows = lax.broadcasted_iota(jnp.int32, (8 * BLOCKS, 4 * SHARD_CH), 0)
+    columns = lax.broadcasted_iota(jnp.int32, (8 * BLOCKS, 4 * SHARD_CH), 1)
+    s, j, half = (rows >> 2) & 1, (rows >> 1) & 1, rows & 1
+    wanted = ((2 * s + half) << 7) + (j << 6) + (rows >> 3)
+    return jnp.where(columns == wanted, 1.0, 0.0).astype(bf16)
 
 
 def tables():
@@ -70,14 +67,15 @@
     return copies
 
 
-def pack_kernel(key_in, value_in, grad_in, query_in, taps_in, order_in, out_ref, *scratch):
+def pack_kernel(key_in, value_in, grad_in, query_in, taps_in, out_ref, *scratch):
     *held, done = scratch
-    key_ref, value_ref, grad_ref, query_ref, taps_ref, order_ref = held
-    sources = (key_in, value_in, grad_in, query_in, taps_in, order_in)
-    for copy in fetch(zip(sources, held, strict=True), done):
+    key_ref, value_ref, grad_ref, query_ref, taps_ref = held
+    sources = (key_in, value_in, grad_in, query_in, taps_in)
+    copies = fetch(zip(sources, held, strict=True), done)
+    order = pack_order()
+    for copy in copies:
         copy.wait()
     taps_high, taps_low = split(taps_ref[...])
-    order = order_ref[...]
 
     def tile(first, second):
         wide = jnp.concatenate(
@@ -290,12 +288,12 @@
     half = BLOCK_LEN // 2
     near_low = lax.ppermute(layer_input[half:], "x", pairs)
     far_high = lax.ppermute(layer_input[:half], "x", rings)
-    sources = (key_gate, value_field, out_grad, query_gate, filter_taps, jnp.asarray(pack_order()))
+    sources = (key_gate, value_field, out_grad, query_gate, filter_taps)
     packed = call(
         pack_kernel,
         "pack",
         sources,
-        [HBM] * 6,
+        [HBM] * 5,
         jax.ShapeDtypeStruct((BLOCKS, 24, 128), bf16),
         held_like(sources),
         60,

time: 92.8 us -> 92.6 us (level)
  local copies, waits for them, and re-layouts: 1.51 us -> 2.54 us
  waiting for transfers between devices: 22.3 us -> 21.3 us
    slice x1, local copies, waits for them, and re-layouts: 0.73 us -> 1.76 us  [on_device(): far_high = lax.ppermute(layer_input[:half], 'x', rings)]
    all_to_all x1, waiting for transfers between devices: 11.7 us -> 10.7 us  [on_device(): lax.all_to_all(packed, ('z', 'x', 'core'), split_axis=0, concat_axis=0, t...]
  transfers between devices with their start and end apart: 15 -> 15, of which waited for: 5 -> 5; matrix products, arithmetic and copies ran while one was open for 1% -> 2% of each run, Pallas kernels for 3% -> 3%
where the time goes in v4:
time: 92.6 us; the launch traced here: 92.2 us
  starting transfers between devices  31.7 us (34%)
  blocking collectives  25.4 us (27%)
  waiting for transfers between devices  21.3 us (23%)
  Pallas kernels  10.6 us (11%)
  local copies, waits for them, and re-layouts  2.54 us (3%)
    all_to_all x1, blocking collectives, on_device(): lax.all_to_all(shares, ('z', 'x', 'core'), split_axis=0, concat_axis=0, t...  25.4 us
    all_to_all x1, starting transfers between devices, on_device(): lax.all_to_all(packed, ('z', 'x', 'core'), split_axis=0, concat_axis=0, t...  13 us
    all_to_all x1, waiting for transfers between devices, on_device(): lax.all_to_all(packed, ('z', 'x', 'core'), split_axis=0, concat_axis=0, t...  10.7 us
    pallas_call x4, Pallas kernels, call(): pl.pallas_call(kernel, out_shape=outs, in_specs=[pl.BlockSpec(memory_spac...  10.6 us
    all_to_all x1, starting transfers between devices, on_device(): lax.all_to_all(grads, ('z', 'y'), split_axis=0, concat_axis=0, tiled=True)  6.51 us
    ppermute x7, starting transfers between devices, on_device(): other = [lax.ppermute(block, 'core', [(0, 1), (1, 0)]) for block in own]  5.99 us
    ppermute x1, waiting for transfers between devices, on_device(): across_low = lax.ppermute(near_low, 'x', rings)  3.59 us
    ppermute x1, waiting for transfers between devices, on_device(): far_low = lax.ppermute(held[half:], 'x', rings)  3.54 us
  transfers between devices with their start and end apart: 15, of which 5 were waited for; matrix products, arithmetic and copies ran while one was open for 2% of the time, Pallas kernels for 3%

profile of v4, /device:TPU:1, one launch (start us, length us, event | category | flops | bytes accessed | tf_op | source)
XLA Modules:
  0.0 92.2 jit_solution(2123875167507236553)
XLA Ops:
  0.6 0.0 copy-start
  0.6 2.5 %pack.1 = bf16[64,24,128]{2,1,0:T(8,128)(2,1)} custom-call(bf16[256,128]{1,0:T(8,128)(2,1)} %key_in.1, bf16[256,128]{1,0:T(8,128)(2,1)} %value_in.1, bf16[256,128]{1,0:T(8,128)(2,1)} %grad_in.1, bf16[256,128]{1,0:T(8,128)(2,1)} %query_in.1, f32[256,128]{1,0:T(8,128)} %taps_in.1), custom_call_target="tpu_custom_call" | custom-call | tf_op jit(solution)/shard_map/pack/pallas_call | solution.py:269
  3.2 13.0 %all-to-all-start = ((bf16[64,24,128]{2,1,0:T(8,128)(2,1)}), bf16[64,24,128]{2,1,0:T(8,128)(2,1)S(1)}, u32[]{:S(2)}, u32[]{:S(2)}) async-start(bf16[64,24,128]{2,1,0:T(8,128)(2,1)} %pack.1), calls=%async_computation | async-start | bytes 786432 | tf_op jit(solution)/shard_map/all_to_all | solution.py:301
  16.2 1.8 %fusion.1 = (bf16[128,1024]{1,0:T(8,128)(2,1)}, bf16[128,1024]{1,0:T(8,128)(2,1)S(1)}) fusion(bf16[256,1024]{1,0:T(8,128)(2,1)} %rest_0_.1), kind=kLoop, calls=%fused_computation.1 | loop fusion | bytes 1048576 | tf_op jit(solution)/shard_map/slice | solution.py:290
  17.9 2.6 %collective-permute-start.1 = (bf16[128,1024]{1,0:T(8,128)(2,1)}, bf16[128,1024]{1,0:T(8,128)(2,1)S(1)}, u32[]{:S(2)}, u32[]{:S(2)}) collective-permute-start(bf16[128,1024]{1,0:T(8,128)(2,1)} %get-tuple-element.16), channel_id=1, source_target_pairs={{0,24},{24,0},{8,16},{16,8},{1,25},{25,1},{9,17},{17,9},{2,26},{26... | collective-permute-start | bytes 786440 | tf_op jit(solution)/shard_map/ppermute | solution.py:290
  20.5 0.0 copy-start.1
  20.5 0.0 collective-permute-start
  20.5 10.7 %all-to-all-done.got_ref = bf16[64,24,128]{2,1,0:T(8,128)(2,1)S(1)} async-done(((bf16[64,24,128]{2,1,0:T(8,128)(2,1)}), bf16[64,24,128]{2,1,0:T(8,128)(2,1)S(1)}, u32[]{:S(2)}, u32[]{:S(2)}) %all-to-all-start) | async-done | bytes 393248 | tf_op jit(solution)/shard_map/all_to_all | solution.py:301
  31.2 0.0 copy-done
  31.2 3.0 %conv.1 = (bf16[32,96,128]{2,1,0:T(8,128)(2,1)}, f32[64,8,128]{2,1,0:T(8,128)S(1)}) custom-call(bf16[64,24,128]{2,1,0:T(8,128)(2,1)S(1)} %all-to-all-done.got_ref, bf16[1344,512]{1,0:T(8,128)(2,1)S(1)} %copy-done), custom_call_target="tpu_custom_call" | custom-call | tf_op jit(solution)/shard_map/conv/pallas_call | solution.py:269
  34.2 0.0 collective-permute-done.1.rest_2_
  34.2 0.0 collective-permute-done.rest_1_
  34.3 6.5 %all-to-all-start.1 = ((bf16[32,96,128]{2,1,0:T(8,128)(2,1)}), bf16[32,96,128]{2,1,0:T(8,128)(2,1)}, u32[]{:S(2)}, u32[]{:S(2)}) async-start(bf16[32,96,128]{2,1,0:T(8,128)(2,1)} %get-tuple-element.9), calls=%async_computation.1 | async-start | bytes 1572864 | tf_op jit(solution)/shard_map/all_to_all | solution.py:323
  40.8 0.0 copy-done.1
  40.8 1.1 %collective-permute-start.6 = (bf16[256,1024]{1,0:T(8,128)(2,1)S(1)}, bf16[256,1024]{1,0:T(8,128)(2,1)S(1)}, u32[]{:S(2)}, u32[]{:S(2)}) collective-permute-start(bf16[256,1024]{1,0:T(8,128)(2,1)S(1)} %copy-done.1), channel_id=1, source_target_pairs={{0,4},{4,0},{1,5},{5,1},{2,6},{6,2},{3,7},{7,3},{8,12},{12,8},{9,1... | collective-permute-start | bytes 1572872 | tf_op jit(solution)/shard_map/ppermute | solution.py:322
  41.9 0.1 collective-permute-start.7
  42.0 1.0 %collective-permute-start.5 = (bf16[128,1024]{1,0:T(8,128)(2,1)S(1)}, bf16[128,1024]{1,0:T(8,128)(2,1)S(1)}, u32[]{:S(2)}, u32[]{:S(2)}) collective-permute-start(bf16[128,1024]{1,0:T(8,128)(2,1)S(1)} %collective-permute-done.rest_1_), channel_id=1, source_target_pairs={{0,24},{24,0},{8,16},{16,8},{1,25},{25,1},{9,17},{17,9},{2,26},{26... | collective-permute-start | bytes 786440 | tf_op jit(solution)/shard_map/ppermute | solution.py:320
  43.0 0.0 collective-permute-start.4
  43.0 1.8 %collective-permute-start.3 = (bf16[128,1024]{1,0:T(8,128)(2,1)S(1)}, bf16[128,1024]{1,0:T(8,128)(2,1)S(1)}, u32[]{:S(2)}, u32[]{:S(2)}) collective-permute-start(bf16[128,1024]{1,0:T(8,128)(2,1)S(1)} %get-tuple-element.14), channel_id=1, source_target_pairs={{0,24},{24,0},{8,16},{16,8},{1,25},{25,1},{9,17},{17,9},{2,26},{26... | collective-permute-start | bytes 786440 | tf_op jit(solution)/shard_map/ppermute | solution.py:318
  44.8 0.0 collective-permute-done.6.rest_7_
  44.8 0.0 copy-start.2
  44.8 0.9 collective-permute-start.2
  45.7 0.0 collective-permute-done.7.rest_8_
  45.7 0.0 copy-start.3
  45.7 1.5 %collective-permute-start.8 = (bf16[128,1024]{1,0:T(8,128)(2,1)S(1)}, bf16[128,1024]{1,0:T(8,128)(2,1)S(1)}, u32[]{:S(2)}, u32[]{:S(2)}) collective-permute-start(bf16[128,1024]{1,0:T(8,128)(2,1)S(1)} %collective-permute-done.1.rest_2_), channel_id=1, source_target_pairs={{0,4},{4,0},{1,5},{5,1},{2,6},{6,2},{3,7},{7,3},{8,12},{12,8},{9,1... | collective-permute-start | bytes 786440 | tf_op jit(solution)/shard_map/ppermute | solution.py:322
  47.2 3.6 %collective-permute-done.5.rest_6_ = bf16[128,1024]{1,0:T(8,128)(2,1)S(1)} collective-permute-done((bf16[128,1024]{1,0:T(8,128)(2,1)S(1)}, bf16[128,1024]{1,0:T(8,128)(2,1)S(1)}, u32[]{:S(2)}, u32[]{:S(2)}) %collective-permute-start.5) | collective-permute-done | bytes 262176 | tf_op jit(solution)/shard_map/ppermute | solution.py:320
  50.8 2.0 %collective-permute-start.12 = (bf16[128,1024]{1,0:T(8,128)(2,1)S(1)}, bf16[128,1024]{1,0:T(8,128)(2,1)S(1)}, u32[]{:S(2)}, u32[]{:S(2)}) collective-permute-start(bf16[128,1024]{1,0:T(8,128)(2,1)S(1)} %collective-permute-done.5.rest_6_), channel_id=1, source_target_pairs={{0,4},{4,0},{1,5},{5,1},{2,6},{6,2},{3,7},{7,3},{8,12},{12,8},{9,1... | collective-permute-start | bytes 786440 | tf_op jit(solution)/shard_map/ppermute | solution.py:322
  52.8 0.0 collective-permute-done.4.rest_5_
  52.8 0.1 collective-permute-start.11
  52.9 3.5 %collective-permute-done.3.rest_4_ = bf16[128,1024]{1,0:T(8,128)(2,1)S(1)} collective-permute-done((bf16[128,1024]{1,0:T(8,128)(2,1)S(1)}, bf16[128,1024]{1,0:T(8,128)(2,1)S(1)}, u32[]{:S(2)}, u32[]{:S(2)}) %collective-permute-start.3) | collective-permute-done | bytes 262176 | tf_op jit(solution)/shard_map/ppermute | solution.py:318
  56.4 1.1 %collective-permute-start.10 = (bf16[128,1024]{1,0:T(8,128)(2,1)S(1)}, bf16[128,1024]{1,0:T(8,128)(2,1)S(1)}, u32[]{:S(2)}, u32[]{:S(2)}) collective-permute-start(bf16[128,1024]{1,0:T(8,128)(2,1)S(1)} %collective-permute-done.3.rest_4_), channel_id=1, source_target_pairs={{0,4},{4,0},{1,5},{5,1},{2,6},{6,2},{3,7},{7,3},{8,12},{12,8},{9,1... | collective-permute-start | bytes 786440 | tf_op jit(solution)/shard_map/ppermute | solution.py:322
  57.6 0.0 collective-permute-done.2.rest_3_
  57.6 0.0 collective-permute-start.9
  57.6 0.0 collective-permute-done.8.rest_9_
  57.6 0.0 copy-start.4
  57.6 0.0 collective-permute-done.12.rest_13_
  57.6 0.0 copy-start.5
  57.6 0.0 collective-permute-done.11.rest_12_
  57.6 0.0 copy-start.6
  57.6 1.4 %collective-permute-done.10.rest_11_ = bf16[128,1024]{1,0:T(8,128)(2,1)S(1)} collective-permute-done((bf16[128,1024]{1,0:T(8,128)(2,1)S(1)}, bf16[128,1024]{1,0:T(8,128)(2,1)S(1)}, u32[]{:S(2)}, u32[]{:S(2)}) %collective-permute-start.10) | collective-permute-done | bytes 262176 | tf_op jit(solution)/shard_map/ppermute | solution.py:322
  59.0 0.0 copy-start.7
  59.0 0.7 copy-done.7
  59.7 0.0 collective-permute-done.9.rest_10_
  59.7 2.1 %all-to-all-done.1.got_in = bf16[32,96,128]{2,1,0:T(8,128)(2,1)} async-done(((bf16[32,96,128]{2,1,0:T(8,128)(2,1)}), bf16[32,96,128]{2,1,0:T(8,128)(2,1)}, u32[]{:S(2)}, u32[]{:S(2)}) %all-to-all-start.1) | async-done | bytes 786464 | tf_op jit(solution)/shard_map/all_to_all | solution.py:323
  61.8 0.0 copy-done.2
  61.8 0.0 copy-done.3
  61.8 0.0 copy-done.4
  61.8 0.0 copy-done.5
  61.8 0.0 copy-done.6
  61.8 4.1 %share.1 = bf16[64,32,128]{2,1,0:T(8,128)(2,1)} custom-call(bf16[32,96,128]{2,1,0:T(8,128)(2,1)} %all-to-all-done.1.got_in, f32[64,8,128]{2,1,0:T(8,128)S(1)} %get-tuple-element.10.lag_in, bf16[256,1024]{1,0:T(8,128)(2,1)} %rest_0_.1, bf16[128,1024]{1,0:T(8,128)(2,1)S(1)} %collective-permute-done.rest_1_, ...), custom_call_target="tpu_custom_call" | custom-call | tf_op jit(solution)/shard_map/share/pallas_call | solution.py:269
  66.0 25.4 %all_to_all.15.got_ref = bf16[64,32,128]{2,1,0:T(8,128)(2,1)S(1)} all-to-all(bf16[64,32,128]{2,1,0:T(8,128)(2,1)} %share.1), channel_id=1, replica_groups=mesh['z'=8,'x'=4,'core'=2,'y'=4] {'z','x','core'}, dimensions={0} | all-to-all | bytes 1048576 | tf_op jit(solution)/shard_map/all_to_all | solution.py:340
  91.3 0.9 finish.1
  (1 shorter events, 0.0 us)
Async XLA Ops:
  0.6 30.6 %copy-start = (bf16[1344,512]{1,0:T(8,128)(2,1)S(1)}, bf16[1344,512]{1,0:T(8,128)(2,1)}, u32[]{:S(2)}) copy-start(bf16[1344,512]{1,0:T(8,128)(2,1)} %constant.2.clone.table_ref) | copy-start | bytes 4128772
  3.2 28.1 %all-to-all-start = ((bf16[64,24,128]{2,1,0:T(8,128)(2,1)}), bf16[64,24,128]{2,1,0:T(8,128)(2,1)S(1)}, u32[]{:S(2)}, u32[]{:S(2)}) async-start(bf16[64,24,128]{2,1,0:T(8,128)(2,1)} %pack.1), calls=%async_computation | async-start | bytes 786432 | tf_op jit(solution)/shard_map/all_to_all | solution.py:301
  17.9 16.3 %collective-permute-start.1 = (bf16[128,1024]{1,0:T(8,128)(2,1)}, bf16[128,1024]{1,0:T(8,128)(2,1)S(1)}, u32[]{:S(2)}, u32[]{:S(2)}) collective-permute-start(bf16[128,1024]{1,0:T(8,128)(2,1)} %get-tuple-element.16), channel_id=1, source_target_pairs={{0,24},{24,0},{8,16},{16,8},{1,25},{25,1},{9,17},{17,9},{2,26},{26... | collective-permute-start | bytes 786440 | tf_op jit(solution)/shard_map/ppermute | solution.py:290
  20.5 20.3 %copy-start.1 = (bf16[256,1024]{1,0:T(8,128)(2,1)S(1)}, bf16[256,1024]{1,0:T(8,128)(2,1)}, u32[]{:S(2)}) copy-start(bf16[256,1024]{1,0:T(8,128)(2,1)} %rest_0_.1) | copy-start | bytes 1572868
  20.5 13.7 %collective-permute-start = (bf16[128,1024]{1,0:T(8,128)(2,1)S(1)}, bf16[128,1024]{1,0:T(8,128)(2,1)S(1)}, u32[]{:S(2)}, u32[]{:S(2)}) collective-permute-start(bf16[128,1024]{1,0:T(8,128)(2,1)S(1)} %get-tuple-element.17), channel_id=1, source_target_pairs={{0,8},{8,0},{16,24},{24,16},{1,9},{9,1},{17,25},{25,17},{2,10},{10... | collective-permute-start | bytes 786440 | tf_op jit(solution)/shard_map/ppermute | solution.py:289
  34.3 27.5 %all-to-all-start.1 = ((bf16[32,96,128]{2,1,0:T(8,128)(2,1)}), bf16[32,96,128]{2,1,0:T(8,128)(2,1)}, u32[]{:S(2)}, u32[]{:S(2)}) async-start(bf16[32,96,128]{2,1,0:T(8,128)(2,1)} %get-tuple-element.9), calls=%async_computation.1 | async-start | bytes 1572864 | tf_op jit(solution)/shard_map/all_to_all | solution.py:323
  40.8 4.1 %collective-permute-start.6 = (bf16[256,1024]{1,0:T(8,128)(2,1)S(1)}, bf16[256,1024]{1,0:T(8,128)(2,1)S(1)}, u32[]{:S(2)}, u32[]{:S(2)}) collective-permute-start(bf16[256,1024]{1,0:T(8,128)(2,1)S(1)} %copy-done.1), channel_id=1, source_target_pairs={{0,4},{4,0},{1,5},{5,1},{2,6},{6,2},{3,7},{7,3},{8,12},{12,8},{9,1... | collective-permute-start | bytes 1572872 | tf_op jit(solution)/shard_map/ppermute | solution.py:322
  41.9 3.8 %collective-permute-start.7 = (bf16[128,1024]{1,0:T(8,128)(2,1)S(1)}, bf16[128,1024]{1,0:T(8,128)(2,1)S(1)}, u32[]{:S(2)}, u32[]{:S(2)}) collective-permute-start(bf16[128,1024]{1,0:T(8,128)(2,1)S(1)} %collective-permute-done.rest_1_), channel_id=1, source_target_pairs={{0,4},{4,0},{1,5},{5,1},{2,6},{6,2},{3,7},{7,3},{8,12},{12,8},{9,1... | collective-permute-start | bytes 786440 | tf_op jit(solution)/shard_map/ppermute | solution.py:322
  42.0 8.8 %collective-permute-start.5 = (bf16[128,1024]{1,0:T(8,128)(2,1)S(1)}, bf16[128,1024]{1,0:T(8,128)(2,1)S(1)}, u32[]{:S(2)}, u32[]{:S(2)}) collective-permute-start(bf16[128,1024]{1,0:T(8,128)(2,1)S(1)} %collective-permute-done.rest_1_), channel_id=1, source_target_pairs={{0,24},{24,0},{8,16},{16,8},{1,25},{25,1},{9,17},{17,9},{2,26},{26... | collective-permute-start | bytes 786440 | tf_op jit(solution)/shard_map/ppermute | solution.py:320
  43.0 9.8 %collective-permute-start.4 = (bf16[128,1024]{1,0:T(8,128)(2,1)S(1)}, bf16[128,1024]{1,0:T(8,128)(2,1)S(1)}, u32[]{:S(2)}, u32[]{:S(2)}) collective-permute-start(bf16[128,1024]{1,0:T(8,128)(2,1)S(1)} %collective-permute-done.1.rest_2_), channel_id=1, source_target_pairs={{0,8},{8,0},{16,24},{24,16},{1,9},{9,1},{17,25},{25,17},{2,10},{10... | collective-permute-start | bytes 786440 | tf_op jit(solution)/shard_map/ppermute | solution.py:319
  43.0 13.4 %collective-permute-start.3 = (bf16[128,1024]{1,0:T(8,128)(2,1)S(1)}, bf16[128,1024]{1,0:T(8,128)(2,1)S(1)}, u32[]{:S(2)}, u32[]{:S(2)}) collective-permute-start(bf16[128,1024]{1,0:T(8,128)(2,1)S(1)} %get-tuple-element.14), channel_id=1, source_target_pairs={{0,24},{24,0},{8,16},{16,8},{1,25},{25,1},{9,17},{17,9},{2,26},{26... | collective-permute-start | bytes 786440 | tf_op jit(solution)/shard_map/ppermute | solution.py:318
  44.8 17.0 %copy-start.2 = (bf16[256,1024]{1,0:T(8,128)(2,1)}, bf16[256,1024]{1,0:T(8,128)(2,1)S(1)}, u32[]{:S(2)}) copy-start(bf16[256,1024]{1,0:T(8,128)(2,1)S(1)} %collective-permute-done.6.rest_7_) | copy-start | bytes 1572868
  44.8 12.7 %collective-permute-start.2 = (bf16[128,1024]{1,0:T(8,128)(2,1)S(1)}, bf16[128,1024]{1,0:T(8,128)(2,1)S(1)}, u32[]{:S(2)}, u32[]{:S(2)}) collective-permute-start(bf16[128,1024]{1,0:T(8,128)(2,1)S(1)} %get-tuple-element.15), channel_id=1, source_target_pairs={{0,8},{8,0},{16,24},{24,16},{1,9},{9,1},{17,25},{25,17},{2,10},{10... | collective-permute-start | bytes 786440 | tf_op jit(solution)/shard_map/ppermute | solution.py:317
  45.7 16.1 %copy-start.3 = (bf16[128,1024]{1,0:T(8,128)(2,1)}, bf16[128,1024]{1,0:T(8,128)(2,1)S(1)}, u32[]{:S(2)}) copy-start(bf16[128,1024]{1,0:T(8,128)(2,1)S(1)} %collective-permute-done.7.rest_8_) | copy-start | bytes 786436
  45.7 11.9 %collective-permute-start.8 = (bf16[128,1024]{1,0:T(8,128)(2,1)S(1)}, bf16[128,1024]{1,0:T(8,128)(2,1)S(1)}, u32[]{:S(2)}, u32[]{:S(2)}) collective-permute-start(bf16[128,1024]{1,0:T(8,128)(2,1)S(1)} %collective-permute-done.1.rest_2_), channel_id=1, source_target_pairs={{0,4},{4,0},{1,5},{5,1},{2,6},{6,2},{3,7},{7,3},{8,12},{12,8},{9,1... | collective-permute-start | bytes 786440 | tf_op jit(solution)/shard_map/ppermute | solution.py:322
  50.8 6.8 %collective-permute-start.12 = (bf16[128,1024]{1,0:T(8,128)(2,1)S(1)}, bf16[128,1024]{1,0:T(8,128)(2,1)S(1)}, u32[]{:S(2)}, u32[]{:S(2)}) collective-permute-start(bf16[128,1024]{1,0:T(8,128)(2,1)S(1)} %collective-permute-done.5.rest_6_), channel_id=1, source_target_pairs={{0,4},{4,0},{1,5},{5,1},{2,6},{6,2},{3,7},{7,3},{8,12},{12,8},{9,1... | collective-permute-start | bytes 786440 | tf_op jit(solution)/shard_map/ppermute | solution.py:322
  52.8 4.8 %collective-permute-start.11 = (bf16[128,1024]{1,0:T(8,128)(2,1)S(1)}, bf16[128,1024]{1,0:T(8,128)(2,1)S(1)}, u32[]{:S(2)}, u32[]{:S(2)}) collective-permute-start(bf16[128,1024]{1,0:T(8,128)(2,1)S(1)} %collective-permute-done.4.rest_5_), channel_id=1, source_target_pairs={{0,4},{4,0},{1,5},{5,1},{2,6},{6,2},{3,7},{7,3},{8,12},{12,8},{9,1... | collective-permute-start | bytes 786440 | tf_op jit(solution)/shard_map/ppermute | solution.py:322
  56.4 2.6 %collective-permute-start.10 = (bf16[128,1024]{1,0:T(8,128)(2,1)S(1)}, bf16[128,1024]{1,0:T(8,128)(2,1)S(1)}, u32[]{:S(2)}, u32[]{:S(2)}) collective-permute-start(bf16[128,1024]{1,0:T(8,128)(2,1)S(1)} %collective-permute-done.3.rest_4_), channel_id=1, source_target_pairs={{0,4},{4,0},{1,5},{5,1},{2,6},{6,2},{3,7},{7,3},{8,12},{12,8},{9,1... | collective-permute-start | bytes 786440 | tf_op jit(solution)/shard_map/ppermute | solution.py:322
  57.6 2.2 %collective-permute-start.9 = (bf16[128,1024]{1,0:T(8,128)(2,1)S(1)}, bf16[128,1024]{1,0:T(8,128)(2,1)}, u32[]{:S(2)}, u32[]{:S(2)}) collective-permute-start(bf16[128,1024]{1,0:T(8,128)(2,1)S(1)} %collective-permute-done.2.rest_3_), channel_id=1, source_target_pairs={{0,4},{4,0},{1,5},{5,1},{2,6},{6,2},{3,7},{7,3},{8,12},{12,8},{9,1... | collective-permute-start | bytes 786440 | tf_op jit(solution)/shard_map/ppermute | solution.py:322
  57.6 4.2 %copy-start.4 = (bf16[128,1024]{1,0:T(8,128)(2,1)}, bf16[128,1024]{1,0:T(8,128)(2,1)S(1)}, u32[]{:S(2)}) copy-start(bf16[128,1024]{1,0:T(8,128)(2,1)S(1)} %collective-permute-done.8.rest_9_) | copy-start | bytes 786436
  57.6 4.2 %copy-start.5 = (bf16[128,1024]{1,0:T(8,128)(2,1)}, bf16[128,1024]{1,0:T(8,128)(2,1)S(1)}, u32[]{:S(2)}) copy-start(bf16[128,1024]{1,0:T(8,128)(2,1)S(1)} %collective-permute-done.12.rest_13_) | copy-start | bytes 786436
  57.6 4.2 %copy-start.6 = (bf16[128,1024]{1,0:T(8,128)(2,1)}, bf16[128,1024]{1,0:T(8,128)(2,1)S(1)}, u32[]{:S(2)}) copy-start(bf16[128,1024]{1,0:T(8,128)(2,1)S(1)} %collective-permute-done.11.rest_12_) | copy-start | bytes 786436
  59.0 0.7 copy-start.7

commit v5 on v4

--- a/solution.py
+++ b/solution.py
@@ -68,7 +68,7 @@
 
 
 def pack_kernel(key_in, value_in, grad_in, query_in, taps_in, out_ref, *scratch):
-    *held, done = scratch
+    *held, done, packed_ref, left = scratch
     key_ref, value_ref, grad_ref, query_ref, taps_ref = held
     sources = (key_in, value_in, grad_in, query_in, taps_in)
     copies = fetch(zip(sources, held, strict=True), done)
@@ -77,20 +77,25 @@
         copy.wait()
     taps_high, taps_low = split(taps_ref[...])
 
-    def tile(first, second):
-        wide = jnp.concatenate(
-            [first[:128], first[128:], second[:128], second[128:]], axis=1
-        )
-        return product(order, wide, ((1,), (1,))).reshape(BLOCKS, 8, 128)
-
-    out_ref[...] = jnp.concatenate(
-        [
-            tile(key_ref[...], value_ref[...]),
-            tile(grad_ref[...], query_ref[...]),
-            tile(taps_high, taps_low),
-        ],
-        axis=1,
-    ).astype(bf16)
+    def wide(first, second):
+        return jnp.concatenate([first[:128], first[128:], second[:128], second[128:]], axis=1)
+
+    fields = (
+        wide(key_ref[...], value_ref[...]),
+        wide(grad_ref[...], query_ref[...]),
+        wide(taps_high, taps_low),
+    )
+    leaving = []
+    for part in range(2):
+        rows = order[256 * part : 256 * part + 256]
+        tiles = [product(rows, field, ((1,), (1,))).reshape(32, 8, 128) for field in fields]
+        blocks = pl.ds(32 * part, 32)
+        packed_ref[blocks] = jnp.concatenate(tiles, axis=1).astype(bf16)
+        copy = pltpu.make_async_copy(packed_ref.at[blocks], out_ref.at[blocks], left.at[part])
+        copy.start()
+        leaving.append(copy)
+    for copy in leaving:
+        copy.wait()
 
 
 def conv_kernel(got_ref, table_ref, out_ref, lag_ref, rows_ref, lag_rows_ref):
@@ -265,12 +270,12 @@
 VMEM, HBM = pltpu.VMEM, pltpu.HBM
 
 
-def call(kernel, name, args, spaces, outs, scratch, grant):
+def call(kernel, name, args, spaces, outs, scratch, grant, places=VMEM):
     return pl.pallas_call(
         kernel,
         out_shape=outs,
         in_specs=[pl.BlockSpec(memory_space=space) for space in spaces],
-        out_specs=jax.tree.map(lambda _: pl.BlockSpec(memory_space=VMEM), outs),
+        out_specs=jax.tree.map(lambda _: pl.BlockSpec(memory_space=places), outs),
         scratch_shapes=scratch,
         compiler_params=pltpu.CompilerParams(vmem_limit_bytes=grant * 2**20),
         name=name,
@@ -295,8 +300,10 @@
         sources,
         [HBM] * 5,
         jax.ShapeDtypeStruct((BLOCKS, 24, 128), bf16),
-        held_like(sources),
+        held_like(sources)
+        + [VMEM((BLOCKS, 24, 128), bf16), pltpu.SemaphoreType.DMA((2,))],
         60,
+        pl.ANY,
     )
     fields = lax.all_to_all(packed, ("z", "x", "core"), split_axis=0, concat_axis=0, tiled=True)
     grads, lags = call(

time: 92.6 us -> 92.5 us (level)
  no operation moved by 1% of the time
where the time goes in v5:
time: 92.5 us; the launch traced here: 92.2 us
  starting transfers between devices  31.7 us (34%)
  blocking collectives  25.4 us (27%)
  waiting for transfers between devices  21.3 us (23%)
  Pallas kernels  10.5 us (11%)
  local copies, waits for them, and re-layouts  2.54 us (3%)
    all_to_all x1, blocking collectives, on_device(): lax.all_to_all(shares, ('z', 'x', 'core'), split_axis=0, concat_axis=0, t...  25.4 us
    all_to_all x1, starting transfers between devices, on_device(): lax.all_to_all(packed, ('z', 'x', 'core'), split_axis=0, concat_axis=0, t...  13 us
    all_to_all x1, waiting for transfers between devices, on_device(): lax.all_to_all(packed, ('z', 'x', 'core'), split_axis=0, concat_axis=0, t...  10.7 us
    pallas_call x4, Pallas kernels, call(): pl.pallas_call(kernel, out_shape=outs, in_specs=[pl.BlockSpec(memory_spac...  10.5 us
    all_to_all x1, starting transfers between devices, on_device(): lax.all_to_all(grads, ('z', 'y'), split_axis=0, concat_axis=0, tiled=True)  6.51 us
    ppermute x7, starting transfers between devices, on_device(): other = [lax.ppermute(block, 'core', [(0, 1), (1, 0)]) for block in own]  5.99 us
    ppermute x1, waiting for transfers between devices, on_device(): across_low = lax.ppermute(near_low, 'x', rings)  3.59 us
    ppermute x1, waiting for transfers between devices, on_device(): far_low = lax.ppermute(held[half:], 'x', rings)  3.55 us
  transfers between devices with their start and end apart: 15, of which 5 were waited for; matrix products, arithmetic and copies ran while one was open for 2% of the time, Pallas kernels for 3%

profile of v5, /device:TPU:1, one launch (start us, length us, event | category | flops | bytes accessed | tf_op | source)
XLA Modules:
  0.0 92.2 jit_solution(14720280821174970915)
XLA Ops:
  0.6 0.0 copy-start
  0.6 2.4 %pack.1 = bf16[64,24,128]{2,1,0:T(8,128)(2,1)} custom-call(bf16[256,128]{1,0:T(8,128)(2,1)} %key_in.1, bf16[256,128]{1,0:T(8,128)(2,1)} %value_in.1, bf16[256,128]{1,0:T(8,128)(2,1)} %grad_in.1, bf16[256,128]{1,0:T(8,128)(2,1)} %query_in.1, f32[256,128]{1,0:T(8,128)} %taps_in.1), custom_call_target="tpu_custom_call" | custom-call | tf_op jit(solution)/shard_map/pack/pallas_call | solution.py:274
  3.1 13.0 %all-to-all-start = ((bf16[64,24,128]{2,1,0:T(8,128)(2,1)}), bf16[64,24,128]{2,1,0:T(8,128)(2,1)S(1)}, u32[]{:S(2)}, u32[]{:S(2)}) async-start(bf16[64,24,128]{2,1,0:T(8,128)(2,1)} %pack.1), calls=%async_computation | async-start | bytes 786432 | tf_op jit(solution)/shard_map/all_to_all | solution.py:308
  16.1 1.8 %fusion.1 = (bf16[128,1024]{1,0:T(8,128)(2,1)}, bf16[128,1024]{1,0:T(8,128)(2,1)S(1)}) fusion(bf16[256,1024]{1,0:T(8,128)(2,1)} %rest_0_.1), kind=kLoop, calls=%fused_computation.1 | loop fusion | bytes 1048576 | tf_op jit(solution)/shard_map/slice | solution.py:295
  17.9 2.6 %collective-permute-start.1 = (bf16[128,1024]{1,0:T(8,128)(2,1)}, bf16[128,1024]{1,0:T(8,128)(2,1)S(1)}, u32[]{:S(2)}, u32[]{:S(2)}) collective-permute-start(bf16[128,1024]{1,0:T(8,128)(2,1)} %get-tuple-element.16), channel_id=1, source_target_pairs={{0,24},{24,0},{8,16},{16,8},{1,25},{25,1},{9,17},{17,9},{2,26},{26... | collective-permute-start | bytes 786440 | tf_op jit(solution)/shard_map/ppermute | solution.py:295
  20.5 0.0 copy-start.1
  20.5 0.0 collective-permute-start
  20.5 10.7 %all-to-all-done.got_ref = bf16[64,24,128]{2,1,0:T(8,128)(2,1)S(1)} async-done(((bf16[64,24,128]{2,1,0:T(8,128)(2,1)}), bf16[64,24,128]{2,1,0:T(8,128)(2,1)S(1)}, u32[]{:S(2)}, u32[]{:S(2)}) %all-to-all-start) | async-done | bytes 393248 | tf_op jit(solution)/shard_map/all_to_all | solution.py:308
  31.2 0.0 copy-done
  31.2 3.0 %conv.1 = (bf16[32,96,128]{2,1,0:T(8,128)(2,1)}, f32[64,8,128]{2,1,0:T(8,128)S(1)}) custom-call(bf16[64,24,128]{2,1,0:T(8,128)(2,1)S(1)} %all-to-all-done.got_ref, bf16[1344,512]{1,0:T(8,128)(2,1)S(1)} %copy-done), custom_call_target="tpu_custom_call" | custom-call | tf_op jit(solution)/shard_map/conv/pallas_call | solution.py:274
  34.2 0.0 collective-permute-done.1.rest_2_
  34.2 0.0 collective-permute-done.rest_1_
  34.2 6.5 %all-to-all-start.1 = ((bf16[32,96,128]{2,1,0:T(8,128)(2,1)}), bf16[32,96,128]{2,1,0:T(8,128)(2,1)}, u32[]{:S(2)}, u32[]{:S(2)}) async-start(bf16[32,96,128]{2,1,0:T(8,128)(2,1)} %get-tuple-element.9), calls=%async_computation.1 | async-start | bytes 1572864 | tf_op jit(solution)/shard_map/all_to_all | solution.py:330
  40.7 0.0 copy-done.1
  40.7 1.2 %collective-permute-start.6 = (bf16[256,1024]{1,0:T(8,128)(2,1)S(1)}, bf16[256,1024]{1,0:T(8,128)(2,1)S(1)}, u32[]{:S(2)}, u32[]{:S(2)}) collective-permute-start(bf16[256,1024]{1,0:T(8,128)(2,1)S(1)} %copy-done.1), channel_id=1, source_target_pairs={{0,4},{4,0},{1,5},{5,1},{2,6},{6,2},{3,7},{7,3},{8,12},{12,8},{9,1... | collective-permute-start | bytes 1572872 | tf_op jit(solution)/shard_map/ppermute | solution.py:329
  41.9 0.1 collective-permute-start.7
  42.0 1.0 %collective-permute-start.5 = (bf16[128,1024]{1,0:T(8,128)(2,1)S(1)}, bf16[128,1024]{1,0:T(8,128)(2,1)S(1)}, u32[]{:S(2)}, u32[]{:S(2)}) collective-permute-start(bf16[128,1024]{1,0:T(8,128)(2,1)S(1)} %collective-permute-done.rest_1_), channel_id=1, source_target_pairs={{0,24},{24,0},{8,16},{16,8},{1,25},{25,1},{9,17},{17,9},{2,26},{26... | collective-permute-start | bytes 786440 | tf_op jit(solution)/shard_map/ppermute | solution.py:327
  42.9 0.0 collective-permute-start.4
  43.0 1.8 %collective-permute-start.3 = (bf16[128,1024]{1,0:T(8,128)(2,1)S(1)}, bf16[128,1024]{1,0:T(8,128)(2,1)S(1)}, u32[]{:S(2)}, u32[]{:S(2)}) collective-permute-start(bf16[128,1024]{1,0:T(8,128)(2,1)S(1)} %get-tuple-element.14), channel_id=1, source_target_pairs={{0,24},{24,0},{8,16},{16,8},{1,25},{25,1},{9,17},{17,9},{2,26},{26... | collective-permute-start | bytes 786440 | tf_op jit(solution)/shard_map/ppermute | solution.py:325
  44.8 0.0 collective-permute-done.6.rest_7_
  44.8 0.0 copy-start.2
  44.8 0.9 collective-permute-start.2
  45.6 0.0 collective-permute-done.7.rest_8_
  45.6 0.0 copy-start.3
  45.6 1.5 %collective-permute-start.8 = (bf16[128,1024]{1,0:T(8,128)(2,1)S(1)}, bf16[128,1024]{1,0:T(8,128)(2,1)S(1)}, u32[]{:S(2)}, u32[]{:S(2)}) collective-permute-start(bf16[128,1024]{1,0:T(8,128)(2,1)S(1)} %collective-permute-done.1.rest_2_), channel_id=1, source_target_pairs={{0,4},{4,0},{1,5},{5,1},{2,6},{6,2},{3,7},{7,3},{8,12},{12,8},{9,1... | collective-permute-start | bytes 786440 | tf_op jit(solution)/shard_map/ppermute | solution.py:329
  47.2 3.6 %collective-permute-done.5.rest_6_ = bf16[128,1024]{1,0:T(8,128)(2,1)S(1)} collective-permute-done((bf16[128,1024]{1,0:T(8,128)(2,1)S(1)}, bf16[128,1024]{1,0:T(8,128)(2,1)S(1)}, u32[]{:S(2)}, u32[]{:S(2)}) %collective-permute-start.5) | collective-permute-done | bytes 262176 | tf_op jit(solution)/shard_map/ppermute | solution.py:327
  50.8 2.0 %collective-permute-start.12 = (bf16[128,1024]{1,0:T(8,128)(2,1)S(1)}, bf16[128,1024]{1,0:T(8,128)(2,1)S(1)}, u32[]{:S(2)}, u32[]{:S(2)}) collective-permute-start(bf16[128,1024]{1,0:T(8,128)(2,1)S(1)} %collective-permute-done.5.rest_6_), channel_id=1, source_target_pairs={{0,4},{4,0},{1,5},{5,1},{2,6},{6,2},{3,7},{7,3},{8,12},{12,8},{9,1... | collective-permute-start | bytes 786440 | tf_op jit(solution)/shard_map/ppermute | solution.py:329
  52.7 0.0 collective-permute-done.4.rest_5_
  52.7 0.1 collective-permute-start.11
  52.8 3.5 %collective-permute-done.3.rest_4_ = bf16[128,1024]{1,0:T(8,128)(2,1)S(1)} collective-permute-done((bf16[128,1024]{1,0:T(8,128)(2,1)S(1)}, bf16[128,1024]{1,0:T(8,128)(2,1)S(1)}, u32[]{:S(2)}, u32[]{:S(2)}) %collective-permute-start.3) | collective-permute-done | bytes 262176 | tf_op jit(solution)/shard_map/ppermute | solution.py:325
  56.4 1.1 %collective-permute-start.10 = (bf16[128,1024]{1,0:T(8,128)(2,1)S(1)}, bf16[128,1024]{1,0:T(8,128)(2,1)S(1)}, u32[]{:S(2)}, u32[]{:S(2)}) collective-permute-start(bf16[128,1024]{1,0:T(8,128)(2,1)S(1)} %collective-permute-done.3.rest_4_), channel_id=1, source_target_pairs={{0,4},{4,0},{1,5},{5,1},{2,6},{6,2},{3,7},{7,3},{8,12},{12,8},{9,1... | collective-permute-start | bytes 786440 | tf_op jit(solution)/shard_map/ppermute | solution.py:329
  57.5 0.0 collective-permute-done.2.rest_3_
  57.5 0.0 collective-permute-start.9
  57.5 0.0 collective-permute-done.8.rest_9_
  57.5 0.0 copy-start.4
  57.5 0.0 collective-permute-done.12.rest_13_
  57.5 0.0 copy-start.5
  57.6 0.0 collective-permute-done.11.rest_12_
  57.6 0.0 copy-start.6
  57.6 1.4 %collective-permute-done.10.rest_11_ = bf16[128,1024]{1,0:T(8,128)(2,1)S(1)} collective-permute-done((bf16[128,1024]{1,0:T(8,128)(2,1)S(1)}, bf16[128,1024]{1,0:T(8,128)(2,1)S(1)}, u32[]{:S(2)}, u32[]{:S(2)}) %collective-permute-start.10) | collective-permute-done | bytes 262176 | tf_op jit(solution)/shard_map/ppermute | solution.py:329
  59.0 0.0 copy-start.7
  59.0 0.7 copy-done.7
  59.7 0.0 collective-permute-done.9.rest_10_
  59.7 2.1 %all-to-all-done.1.got_in = bf16[32,96,128]{2,1,0:T(8,128)(2,1)} async-done(((bf16[32,96,128]{2,1,0:T(8,128)(2,1)}), bf16[32,96,128]{2,1,0:T(8,128)(2,1)}, u32[]{:S(2)}, u32[]{:S(2)}) %all-to-all-start.1) | async-done | bytes 786464 | tf_op jit(solution)/shard_map/all_to_all | solution.py:330
  61.7 0.0 copy-done.2
  61.7 0.0 copy-done.3
  61.7 0.0 copy-done.4
  61.7 0.0 copy-done.5
  61.8 0.0 copy-done.6
  61.8 4.1 %share.1 = bf16[64,32,128]{2,1,0:T(8,128)(2,1)} custom-call(bf16[32,96,128]{2,1,0:T(8,128)(2,1)} %all-to-all-done.1.got_in, f32[64,8,128]{2,1,0:T(8,128)S(1)} %get-tuple-element.10.lag_in, bf16[256,1024]{1,0:T(8,128)(2,1)} %rest_0_.1, bf16[128,1024]{1,0:T(8,128)(2,1)S(1)} %collective-permute-done.rest_1_, ...), custom_call_target="tpu_custom_call" | custom-call | tf_op jit(solution)/shard_map/share/pallas_call | solution.py:274
  65.9 25.4 %all_to_all.15.got_ref = bf16[64,32,128]{2,1,0:T(8,128)(2,1)S(1)} all-to-all(bf16[64,32,128]{2,1,0:T(8,128)(2,1)} %share.1), channel_id=1, replica_groups=mesh['z'=8,'x'=4,'core'=2,'y'=4] {'z','x','core'}, dimensions={0} | all-to-all | bytes 1048576 | tf_op jit(solution)/shard_map/all_to_all | solution.py:347
  91.3 0.9 finish.1
  (1 shorter events, 0.0 us)
Async XLA Ops:
  0.6 30.5 %copy-start = (bf16[1344,512]{1,0:T(8,128)(2,1)S(1)}, bf16[1344,512]{1,0:T(8,128)(2,1)}, u32[]{:S(2)}) copy-start(bf16[1344,512]{1,0:T(8,128)(2,1)} %constant.2.clone.table_ref) | copy-start | bytes 4128772
  3.1 28.1 %all-to-all-start = ((bf16[64,24,128]{2,1,0:T(8,128)(2,1)}), bf16[64,24,128]{2,1,0:T(8,128)(2,1)S(1)}, u32[]{:S(2)}, u32[]{:S(2)}) async-start(bf16[64,24,128]{2,1,0:T(8,128)(2,1)} %pack.1), calls=%async_computation | async-start | bytes 786432 | tf_op jit(solution)/shard_map/all_to_all | solution.py:308
  17.9 16.3 %collective-permute-start.1 = (bf16[128,1024]{1,0:T(8,128)(2,1)}, bf16[128,1024]{1,0:T(8,128)(2,1)S(1)}, u32[]{:S(2)}, u32[]{:S(2)}) collective-permute-start(bf16[128,1024]{1,0:T(8,128)(2,1)} %get-tuple-element.16), channel_id=1, source_target_pairs={{0,24},{24,0},{8,16},{16,8},{1,25},{25,1},{9,17},{17,9},{2,26},{26... | collective-permute-start | bytes 786440 | tf_op jit(solution)/shard_map/ppermute | solution.py:295
  20.5 20.3 %copy-start.1 = (bf16[256,1024]{1,0:T(8,128)(2,1)S(1)}, bf16[256,1024]{1,0:T(8,128)(2,1)}, u32[]{:S(2)}) copy-start(bf16[256,1024]{1,0:T(8,128)(2,1)} %rest_0_.1) | copy-start | bytes 1572868
  20.5 13.7 %collective-permute-start = (bf16[128,1024]{1,0:T(8,128)(2,1)S(1)}, bf16[128,1024]{1,0:T(8,128)(2,1)S(1)}, u32[]{:S(2)}, u32[]{:S(2)}) collective-permute-start(bf16[128,1024]{1,0:T(8,128)(2,1)S(1)} %get-tuple-element.17), channel_id=1, source_target_pairs={{0,8},{8,0},{16,24},{24,16},{1,9},{9,1},{17,25},{25,17},{2,10},{10... | collective-permute-start | bytes 786440 | tf_op jit(solution)/shard_map/ppermute | solution.py:294
  34.2 27.6 %all-to-all-start.1 = ((bf16[32,96,128]{2,1,0:T(8,128)(2,1)}), bf16[32,96,128]{2,1,0:T(8,128)(2,1)}, u32[]{:S(2)}, u32[]{:S(2)}) async-start(bf16[32,96,128]{2,1,0:T(8,128)(2,1)} %get-tuple-element.9), calls=%async_computation.1 | async-start | bytes 1572864 | tf_op jit(solution)/shard_map/all_to_all | solution.py:330
  40.7 4.1 %collective-permute-start.6 = (bf16[256,1024]{1,0:T(8,128)(2,1)S(1)}, bf16[256,1024]{1,0:T(8,128)(2,1)S(1)}, u32[]{:S(2)}, u32[]{:S(2)}) collective-permute-start(bf16[256,1024]{1,0:T(8,128)(2,1)S(1)} %copy-done.1), channel_id=1, source_target_pairs={{0,4},{4,0},{1,5},{5,1},{2,6},{6,2},{3,7},{7,3},{8,12},{12,8},{9,1... | collective-permute-start | bytes 1572872 | tf_op jit(solution)/shard_map/ppermute | solution.py:329
  41.9 3.8 %collective-permute-start.7 = (bf16[128,1024]{1,0:T(8,128)(2,1)S(1)}, bf16[128,1024]{1,0:T(8,128)(2,1)S(1)}, u32[]{:S(2)}, u32[]{:S(2)}) collective-permute-start(bf16[128,1024]{1,0:T(8,128)(2,1)S(1)} %collective-permute-done.rest_1_), channel_id=1, source_target_pairs={{0,4},{4,0},{1,5},{5,1},{2,6},{6,2},{3,7},{7,3},{8,12},{12,8},{9,1... | collective-permute-start | bytes 786440 | tf_op jit(solution)/shard_map/ppermute | solution.py:329
  42.0 8.8 %collective-permute-start.5 = (bf16[128,1024]{1,0:T(8,128)(2,1)S(1)}, bf16[128,1024]{1,0:T(8,128)(2,1)S(1)}, u32[]{:S(2)}, u32[]{:S(2)}) collective-permute-start(bf16[128,1024]{1,0:T(8,128)(2,1)S(1)} %collective-permute-done.rest_1_), channel_id=1, source_target_pairs={{0,24},{24,0},{8,16},{16,8},{1,25},{25,1},{9,17},{17,9},{2,26},{26... | collective-permute-start | bytes 786440 | tf_op jit(solution)/shard_map/ppermute | solution.py:327
  42.9 9.8 %collective-permute-start.4 = (bf16[128,1024]{1,0:T(8,128)(2,1)S(1)}, bf16[128,1024]{1,0:T(8,128)(2,1)S(1)}, u32[]{:S(2)}, u32[]{:S(2)}) collective-permute-start(bf16[128,1024]{1,0:T(8,128)(2,1)S(1)} %collective-permute-done.1.rest_2_), channel_id=1, source_target_pairs={{0,8},{8,0},{16,24},{24,16},{1,9},{9,1},{17,25},{25,17},{2,10},{10... | collective-permute-start | bytes 786440 | tf_op jit(solution)/shard_map/ppermute | solution.py:326
  43.0 13.4 %collective-permute-start.3 = (bf16[128,1024]{1,0:T(8,128)(2,1)S(1)}, bf16[128,1024]{1,0:T(8,128)(2,1)S(1)}, u32[]{:S(2)}, u32[]{:S(2)}) collective-permute-start(bf16[128,1024]{1,0:T(8,128)(2,1)S(1)} %get-tuple-element.14), channel_id=1, source_target_pairs={{0,24},{24,0},{8,16},{16,8},{1,25},{25,1},{9,17},{17,9},{2,26},{26... | collective-permute-start | bytes 786440 | tf_op jit(solution)/shard_map/ppermute | solution.py:325
  44.8 17.0 %copy-start.2 = (bf16[256,1024]{1,0:T(8,128)(2,1)}, bf16[256,1024]{1,0:T(8,128)(2,1)S(1)}, u32[]{:S(2)}) copy-start(bf16[256,1024]{1,0:T(8,128)(2,1)S(1)} %collective-permute-done.6.rest_7_) | copy-start | bytes 1572868
  44.8 12.7 %collective-permute-start.2 = (bf16[128,1024]{1,0:T(8,128)(2,1)S(1)}, bf16[128,1024]{1,0:T(8,128)(2,1)S(1)}, u32[]{:S(2)}, u32[]{:S(2)}) collective-permute-start(bf16[128,1024]{1,0:T(8,128)(2,1)S(1)} %get-tuple-element.15), channel_id=1, source_target_pairs={{0,8},{8,0},{16,24},{24,16},{1,9},{9,1},{17,25},{25,17},{2,10},{10... | collective-permute-start | bytes 786440 | tf_op jit(solution)/shard_map/ppermute | solution.py:324
  45.6 16.1 %copy-start.3 = (bf16[128,1024]{1,0:T(8,128)(2,1)}, bf16[128,1024]{1,0:T(8,128)(2,1)S(1)}, u32[]{:S(2)}) copy-start(bf16[128,1024]{1,0:T(8,128)(2,1)S(1)} %collective-permute-done.7.rest_8_) | copy-start | bytes 786436
  45.6 11.9 %collective-permute-start.8 = (bf16[128,1024]{1,0:T(8,128)(2,1)S(1)}, bf16[128,1024]{1,0:T(8,128)(2,1)S(1)}, u32[]{:S(2)}, u32[]{:S(2)}) collective-permute-start(bf16[128,1024]{1,0:T(8,128)(2,1)S(1)} %collective-permute-done.1.rest_2_), channel_id=1, source_target_pairs={{0,4},{4,0},{1,5},{5,1},{2,6},{6,2},{3,7},{7,3},{8,12},{12,8},{9,1... | collective-permute-start | bytes 786440 | tf_op jit(solution)/shard_map/ppermute | solution.py:329
  50.8 6.8 %collective-permute-start.12 = (bf16[128,1024]{1,0:T(8,128)(2,1)S(1)}, bf16[128,1024]{1,0:T(8,128)(2,1)S(1)}, u32[]{:S(2)}, u32[]{:S(2)}) collective-permute-start(bf16[128,1024]{1,0:T(8,128)(2,1)S(1)} %collective-permute-done.5.rest_6_), channel_id=1, source_target_pairs={{0,4},{4,0},{1,5},{5,1},{2,6},{6,2},{3,7},{7,3},{8,12},{12,8},{9,1... | collective-permute-start | bytes 786440 | tf_op jit(solution)/shard_map/ppermute | solution.py:329
  52.7 4.8 %collective-permute-start.11 = (bf16[128,1024]{1,0:T(8,128)(2,1)S(1)}, bf16[128,1024]{1,0:T(8,128)(2,1)S(1)}, u32[]{:S(2)}, u32[]{:S(2)}) collective-permute-start(bf16[128,1024]{1,0:T(8,128)(2,1)S(1)} %collective-permute-done.4.rest_5_), channel_id=1, source_target_pairs={{0,4},{4,0},{1,5},{5,1},{2,6},{6,2},{3,7},{7,3},{8,12},{12,8},{9,1... | collective-permute-start | bytes 786440 | tf_op jit(solution)/shard_map/ppermute | solution.py:329
  56.4 2.6 %collective-permute-start.10 = (bf16[128,1024]{1,0:T(8,128)(2,1)S(1)}, bf16[128,1024]{1,0:T(8,128)(2,1)S(1)}, u32[]{:S(2)}, u32[]{:S(2)}) collective-permute-start(bf16[128,1024]{1,0:T(8,128)(2,1)S(1)} %collective-permute-done.3.rest_4_), channel_id=1, source_target_pairs={{0,4},{4,0},{1,5},{5,1},{2,6},{6,2},{3,7},{7,3},{8,12},{12,8},{9,1... | collective-permute-start | bytes 786440 | tf_op jit(solution)/shard_map/ppermute | solution.py:329
  57.5 2.2 %collective-permute-start.9 = (bf16[128,1024]{1,0:T(8,128)(2,1)S(1)}, bf16[128,1024]{1,0:T(8,128)(2,1)}, u32[]{:S(2)}, u32[]{:S(2)}) collective-permute-start(bf16[128,1024]{1,0:T(8,128)(2,1)S(1)} %collective-permute-done.2.rest_3_), channel_id=1, source_target_pairs={{0,4},{4,0},{1,5},{5,1},{2,6},{6,2},{3,7},{7,3},{8,12},{12,8},{9,1... | collective-permute-start | bytes 786440 | tf_op jit(solution)/shard_map/ppermute | solution.py:329
  57.5 4.2 %copy-start.4 = (bf16[128,1024]{1,0:T(8,128)(2,1)}, bf16[128,1024]{1,0:T(8,128)(2,1)S(1)}, u32[]{:S(2)}) copy-start(bf16[128,1024]{1,0:T(8,128)(2,1)S(1)} %collective-permute-done.8.rest_9_) | copy-start | bytes 786436
  57.5 4.2 %copy-start.5 = (bf16[128,1024]{1,0:T(8,128)(2,1)}, bf16[128,1024]{1,0:T(8,128)(2,1)S(1)}, u32[]{:S(2)}) copy-start(bf16[128,1024]{1,0:T(8,128)(2,1)S(1)} %collective-permute-done.12.rest_13_) | copy-start | bytes 786436
  57.6 4.2 %copy-start.6 = (bf16[128,1024]{1,0:T(8,128)(2,1)}, bf16[128,1024]{1,0:T(8,128)(2,1)S(1)}, u32[]{:S(2)}) copy-start(bf16[128,1024]{1,0:T(8,128)(2,1)S(1)} %collective-permute-done.11.rest_12_) | copy-start | bytes 786436
  59.0 0.7 copy-start.7
